TPU v7x, 768 devices: a whole 4x8x12 slice. The times are simulated.
768 devices in a mesh: dp: 192 (over y, z_lo, x), width: 4 (over z_hi, core).
Axes of the slice: x: 4, y: 8, z: 12 (z_hi: 2, z_lo: 6; z = z_hi * 6 + z_lo), core: 2. Of those that a mesh axis runs over, the one named last changes fastest.
Arguments:
- image_embed: bfloat16 [73728, 1152], P('dp', 'width'), may hold values from -0.17675781 to 0.17675781
- text_embed: bfloat16 [73728, 1152], P('dp', 'width'), may hold values from -0.17675781 to 0.17675781
- logit_scale: float32 [1], replicated, may hold values from 2 to 8
- logit_bias: float32 [1], replicated, may hold values from -3 to 0
Outputs:
- image_grad: float32 [73728, 1152], P('dp', 'width')
- text_grad: float32 [73728, 1152], P('dp', 'width')
All inputs are finite; a program needn't handle non-finite values.
Results may differ from a plain program's by a relative error of at most 0.0028.
Values may be sent and summed in bfloat16 or wider, within the bound.
No kernel may reach another device: no remote copies, remote signals or barrier semaphores. Data moves between devices by JAX's collectives and lax.ppermute only.
A program may use at most 32 MiB of HBM per device.

v0:
```python
import jax
import jax.numpy as jnp
from jax import lax
from jax.sharding import PartitionSpec as P

STEPS = 4


def from_behind(block, axis, distance):
    devices = range(lax.axis_size(axis))
    route = [((i - distance) % len(devices), i) for i in devices]
    return lax.ppermute(block, axis, route)


def make_target(logits, first):
    lined = lax.broadcasted_iota(jnp.int32, logits.shape, 0)
    column = lax.broadcasted_iota(jnp.int32, logits.shape, 1)
    return jnp.where(jnp.logical_and(first, lined == column), 1.0, 0.0).astype(jnp.float32)


def loss_weights(partial_value, temper, offset, first):
    logits = temper * lax.psum(partial_value, "width") + offset
    target = make_target(logits, first)
    return (temper * (jax.nn.sigmoid(logits) - target)).astype(jnp.bfloat16)


def on_device(image_embed, text_embed, logit_scale, logit_bias):
    temper = logit_scale[0]
    offset = logit_bias[0]
    text_rows = text_embed
    image_total = jnp.zeros((image_embed.shape[0], text_rows.shape[1]), jnp.float32)
    carried = jnp.zeros(text_rows.shape, jnp.float32)
    for step in range(STEPS):
        if step > 0:
            text_rows = from_behind(text_rows, "dp", 1)
        partial_value = lax.dot_general(
            image_embed, text_rows, (((1,), (1,)), ((), ())), preferred_element_type=jnp.float32
        )
        weights = loss_weights(partial_value, temper, offset, step == 0)
        image_total = image_total + jnp.dot(weights, text_rows, preferred_element_type=jnp.float32)
        term = lax.dot_general(
            weights, image_embed, (((0,), (0,)), ((), ())), preferred_element_type=jnp.float32
        )
        if step > 0:
            carried = from_behind(carried, "dp", 1)
        carried = carried + term
    text_total = from_behind(carried, "dp", 1 - STEPS)
    return (image_total, text_total)


def solution(mesh):
    in_specs = (P("dp", "width"), P("dp", "width"), P(), P())
    out_specs = (P("dp", "width"), P("dp", "width"))
    return jax.shard_map(
        on_device, mesh=mesh, in_specs=in_specs, out_specs=out_specs, check_vma=False
    )
```

profile of v0, /device:TPU:1, one launch (start us, length us, event | category | flops | bytes accessed | tf_op | source)
XLA Modules:
  0.0 314.4 jit_solution(8381952460935939837)
XLA Ops:
  7.2 0.0 all-reduce.3.cloned.1.call-start
  7.2 4.1 %collective-permute-start = (bf16[384,288]{0,1:T(8,128)(2,1)}, bf16[384,288]{0,1:T(8,128)(2,1)S(1)}, u32[]{:S(2)}, u32[]{:S(2)}) collective-permute-start(bf16[384,288]{0,1:T(8,128)(2,1)} %param.5), channel_id=1, source_target_pairs={{764,0},{0,4},{4,8},{8,12},{12,16},{16,20},{20,24},{24,28},{28,32}... | collective-permute-start | bytes 663560 | tf_op jit(solution)/shard_map/ppermute | solution.py:12
  11.3 2.2 fusion.2
  13.5 15.8 %collective-permute-done = bf16[384,288]{0,1:T(8,128)(2,1)S(1)} collective-permute-done((bf16[384,288]{0,1:T(8,128)(2,1)}, bf16[384,288]{0,1:T(8,128)(2,1)S(1)}, u32[]{:S(2)}, u32[]{:S(2)}) %collective-permute-start) | collective-permute-done | bytes 221216 | tf_op jit(solution)/shard_map/ppermute | solution.py:12
  29.3 1.9 collective-permute-start.1
  31.2 1.2 fusion.4
  32.3 12.6 %collective-permute-done.1 = bf16[384,288]{0,1:T(8,128)(2,1)S(1)} collective-permute-done((bf16[384,288]{0,1:T(8,128)(2,1)S(1)}, bf16[384,288]{0,1:T(8,128)(2,1)S(1)}, u32[]{:S(2)}, u32[]{:S(2)}) %collective-permute-start.1) | collective-permute-done | bytes 221216 | tf_op jit(solution)/shard_map/ppermute | solution.py:12
  44.9 1.9 collective-permute-start.2
  46.9 1.2 fusion.5
  48.0 12.6 %collective-permute-done.2 = bf16[384,288]{0,1:T(8,128)(2,1)S(1)} collective-permute-done((bf16[384,288]{0,1:T(8,128)(2,1)S(1)}, bf16[384,288]{0,1:T(8,128)(2,1)S(1)}, u32[]{:S(2)}, u32[]{:S(2)}) %collective-permute-start.2) | collective-permute-done | bytes 221216 | tf_op jit(solution)/shard_map/ppermute | solution.py:12
  60.6 1.2 fusion.6
  61.8 0.0 all-reduce.3.cloned.1.call-update
  63.1 165.7 %all-reduce.3.cloned.1.call-done = (f32[384,384]{1,0:T(8,128)}, f32[384,384]{1,0:T(8,128)}, f32[384,384]{1,0:T(8,128)}, f32[384,384]{1,0:T(8,128)}) async-done(((f32[384,384]{1,0:T(8,128)}, f32[384,384]{1,0:T(8,128)}, f32[384,384]{1,0:T(8,128)}, f32[384,384]{1,0:T(8,128)}), (f32[384,384]{1,0:T(8,128)}, f32[384,384]{1,0:T(8,128)}, f32[384,384]{1,0:T(8,128)}, ...) | async-done | bytes 2359312 | tf_op jit(solution)/shard_map/psum | solution.py:22
  228.8 1.3 multiply_convert_fusion.3
  230.1 0.3 fusion.7
  230.4 3.2 %collective-permute-start.3 = (f32[384,288]{0,1:T(8,128)S(1)}, f32[384,288]{0,1:T(8,128)S(1)}, u32[]{:S(2)}, u32[]{:S(2)}) collective-permute-start(f32[384,288]{0,1:T(8,128)S(1)} %fusion.7), channel_id=1, source_target_pairs={{764,0},{0,4},{4,8},{8,12},{12,16},{16,20},{20,24},{24,28},{28,32}... | collective-permute-start | bytes 1327112 | tf_op jit(solution)/shard_map/ppermute | solution.py:12
  233.7 19.1 %collective-permute-done.3 = f32[384,288]{0,1:T(8,128)S(1)} collective-permute-done((f32[384,288]{0,1:T(8,128)S(1)}, f32[384,288]{0,1:T(8,128)S(1)}, u32[]{:S(2)}, u32[]{:S(2)}) %collective-permute-start.3) | collective-permute-done | bytes 442400 | tf_op jit(solution)/shard_map/ppermute | solution.py:12
  252.7 0.4 convolution_add_fusion
  253.1 1.9 collective-permute-start.4
  255.1 0.4 fusion
  255.5 0.6 copy-done.2
  256.1 0.4 fusion.1
  256.5 18.0 %collective-permute-done.4 = f32[384,288]{0,1:T(8,128)S(1)} collective-permute-done((f32[384,288]{0,1:T(8,128)S(1)}, f32[384,288]{0,1:T(8,128)S(1)}, u32[]{:S(2)}, u32[]{:S(2)}) %collective-permute-start.4) | collective-permute-done | bytes 442400 | tf_op jit(solution)/shard_map/ppermute | solution.py:12
  274.6 1.9 collective-permute-start.5
  276.5 0.3 fusion.3
  276.8 0.4 convolution_add_fusion.3
  277.2 17.8 %collective-permute-done.5 = f32[384,288]{0,1:T(8,128)S(1)} collective-permute-done((f32[384,288]{0,1:T(8,128)S(1)}, f32[384,288]{0,1:T(8,128)S(1)}, u32[]{:S(2)}, u32[]{:S(2)}) %collective-permute-start.5) | collective-permute-done | bytes 442400 | tf_op jit(solution)/shard_map/ppermute | solution.py:12
  295.1 1.9 collective-permute-start.6
  297.0 0.4 convolution_add_fusion.2
  297.4 1.2 convolution_add_fusion.1
  298.6 8.2 %collective-permute-done.6 = f32[384,288]{0,1:T(8,128)S(1)} collective-permute-done((f32[384,288]{0,1:T(8,128)S(1)}, f32[384,288]{0,1:T(8,128)S(1)}, u32[]{:S(2)}, u32[]{:S(2)}) %collective-permute-start.6) | collective-permute-done | bytes 442400 | tf_op jit(solution)/shard_map/ppermute | solution.py:12
  306.8 0.8 copy.13
  (11 shorter events, 0.1 us)
Async XLA Ops:
  7.2 4.2 %copy-start = (bf16[384,288]{0,1:T(8,128)(2,1)S(1)}, bf16[384,288]{0,1:T(8,128)(2,1)}, u32[]{:S(2)}) copy-start(bf16[384,288]{0,1:T(8,128)(2,1)} %param.4) | copy-start | bytes 663556
  7.2 221.7 %all-reduce.3.cloned.1.call-start = ((), (), s32[]{:S(2)}) async-start(), calls=%async_computation | async-start | bytes 4718592 | tf_op jit(solution)/shard_map/psum | solution.py:22
  7.2 22.0 %collective-permute-start = (bf16[384,288]{0,1:T(8,128)(2,1)}, bf16[384,288]{0,1:T(8,128)(2,1)S(1)}, u32[]{:S(2)}, u32[]{:S(2)}) collective-permute-start(bf16[384,288]{0,1:T(8,128)(2,1)} %param.5), channel_id=1, source_target_pairs={{764,0},{0,4},{4,8},{8,12},{12,16},{16,20},{20,24},{24,28},{28,32}... | collective-permute-start | bytes 663560 | tf_op jit(solution)/shard_map/ppermute | solution.py:12
  29.3 15.7 %collective-permute-start.1 = (bf16[384,288]{0,1:T(8,128)(2,1)S(1)}, bf16[384,288]{0,1:T(8,128)(2,1)S(1)}, u32[]{:S(2)}, u32[]{:S(2)}) collective-permute-start(bf16[384,288]{0,1:T(8,128)(2,1)S(1)} %collective-permute-done), channel_id=1, source_target_pairs={{764,0},{0,4},{4,8},{8,12},{12,16},{16,20},{20,24},{24,28},{28,32}... | collective-permute-start | bytes 663560 | tf_op jit(solution)/shard_map/ppermute | solution.py:12
  44.9 15.7 %collective-permute-start.2 = (bf16[384,288]{0,1:T(8,128)(2,1)S(1)}, bf16[384,288]{0,1:T(8,128)(2,1)S(1)}, u32[]{:S(2)}, u32[]{:S(2)}) collective-permute-start(bf16[384,288]{0,1:T(8,128)(2,1)S(1)} %collective-permute-done.1), channel_id=1, source_target_pairs={{764,0},{0,4},{4,8},{8,12},{12,16},{16,20},{20,24},{24,28},{28,32}... | collective-permute-start | bytes 663560 | tf_op jit(solution)/shard_map/ppermute | solution.py:12
  230.1 22.6 %copy-start.4 = (f32[384,384]{1,0:T(8,128)S(1)}, f32[384,384]{1,0:T(8,128)}, u32[]{:S(2)}) copy-start(f32[384,384]{1,0:T(8,128)} %get-tuple-element.3) | copy-start | bytes 1769476
  230.4 22.3 %collective-permute-start.3 = (f32[384,288]{0,1:T(8,128)S(1)}, f32[384,288]{0,1:T(8,128)S(1)}, u32[]{:S(2)}, u32[]{:S(2)}) collective-permute-start(f32[384,288]{0,1:T(8,128)S(1)} %fusion.7), channel_id=1, source_target_pairs={{764,0},{0,4},{4,8},{8,12},{12,16},{16,20},{20,24},{24,28},{28,32}... | collective-permute-start | bytes 1327112 | tf_op jit(solution)/shard_map/ppermute | solution.py:12
  252.7 2.3 copy-start.3
  253.1 21.4 %collective-permute-start.4 = (f32[384,288]{0,1:T(8,128)S(1)}, f32[384,288]{0,1:T(8,128)S(1)}, u32[]{:S(2)}, u32[]{:S(2)}) collective-permute-start(f32[384,288]{0,1:T(8,128)S(1)} %convolution_add_fusion), channel_id=1, source_target_pairs={{764,0},{0,4},{4,8},{8,12},{12,16},{16,20},{20,24},{24,28},{28,32}... | collective-permute-start | bytes 1327112 | tf_op jit(solution)/shard_map/ppermute | solution.py:12
  255.1 1.1 copy-start.2
  256.5 20.0 %copy-start.1 = (bf16[384,288]{0,1:T(8,128)(2,1)S(1)}, bf16[384,288]{0,1:T(8,128)(2,1)}, u32[]{:S(2)}) copy-start(bf16[384,288]{0,1:T(8,128)(2,1)} %param.5) | copy-start | bytes 663556
  274.6 20.5 %collective-permute-start.5 = (f32[384,288]{0,1:T(8,128)S(1)}, f32[384,288]{0,1:T(8,128)S(1)}, u32[]{:S(2)}, u32[]{:S(2)}) collective-permute-start(f32[384,288]{0,1:T(8,128)S(1)} %add.69), channel_id=1, source_target_pairs={{764,0},{0,4},{4,8},{8,12},{12,16},{16,20},{20,24},{24,28},{28,32}... | collective-permute-start | bytes 1327112 | tf_op jit(solution)/shard_map/ppermute | solution.py:12
  295.1 11.7 %collective-permute-start.6 = (f32[384,288]{0,1:T(8,128)S(1)}, f32[384,288]{0,1:T(8,128)S(1)}, u32[]{:S(2)}, u32[]{:S(2)}) collective-permute-start(f32[384,288]{0,1:T(8,128)S(1)} %add.70), channel_id=1, source_target_pairs={{12,0},{16,4},{20,8},{24,12},{28,16},{32,20},{36,24},{40,28},{44,3... | collective-permute-start | bytes 1327112 | tf_op jit(solution)/shard_map/ppermute | solution.py:12
Sparse Core Ops, SparseCore 0:
  62.0 166.8 all-reduce.2
where the time goes:
time: 320 us; the launch traced here: 314 us
  waiting for transfers between devices  270 us (84%)
  starting transfers between devices  16.9 us (5%)
  between operations  15.5 us (5%)
  matrix products  9.51 us (3%)
    psum x1, waiting for transfers between devices, loss_weights(): logits = temper * lax.psum(partial_value, 'width') + offset  166 us
    ppermute x7, waiting for transfers between devices, from_behind(): return lax.ppermute(block, axis, route)  104 us
    ppermute x7, starting transfers between devices, from_behind(): return lax.ppermute(block, axis, route)  16.9 us
  transfers between devices with their start and end apart: 8, of which 8 were waited for; matrix products, arithmetic and copies ran while one was open for 2% of the time, Pallas kernels for 0%

commit v1 on v0

v1 whole, which is shorter than its diff:
```python
import numpy as np
import jax
import jax.numpy as jnp
from jax import lax
from jax.experimental import pallas as pl
from jax.experimental.pallas import tpu as pltpu
from jax.sharding import Mesh, PartitionSpec as P

AXES = ("y", "zl", "x", "zh", "core")
SIZES = (8, 6, 4, 2, 2)
NX = 4


def route(move):
    pairs = []
    for i, place in enumerate(np.ndindex(*SIZES)):
        goal = [a % b for a, b in zip(move(*place), SIZES)]
        pairs.append((i, int(np.ravel_multi_index(goal, SIZES))))
    return pairs


def flip(block):
    return lax.ppermute(block, AXES, route(lambda y, zl, x, zh, c: (y, zl, x, 1 - zh, c)))


def swap_cores(block):
    return lax.ppermute(block, AXES, route(lambda y, zl, x, zh, c: (y, zl, x, zh, 1 - c)))


def next_row(y, zl, x, zh, c):
    step = 1 if c == 0 else -1
    z = (zh * 6 + zl + step) % 12
    row = zl + step
    y = y + 1 if row > 5 else y - 1 if row < 0 else y
    return (y, z % 6, x, z // 6, c)


def shift_row(block):
    return lax.ppermute(block, AXES, route(next_row))


def grads_kernel(info, scalars, yo, yc, xo, xc, keep, send, yt):
    m = pl.program_id(0)
    place, row, core = info[0], info[1], info[2]
    temper, offset = scalars[0], scalars[1]
    wrapped = jnp.where(core == 0, jnp.logical_and(m > place, row == 0), jnp.logical_and(m < place, row == 5))
    side = wrapped.astype(jnp.int32)

    @pl.when(m == 0)
    def _():
        yt[0] = yo[...].T
        yt[1] = yc[...].T
        keep[...] = jnp.zeros_like(keep)
        send[...] = jnp.zeros_like(send)

    a, b = xo[0], xc[0]
    logits = jnp.dot(yt[side], a, preferred_element_type=jnp.float32)
    logits += jnp.dot(yt[1 - side], b, preferred_element_type=jnp.float32)
    logits = temper * logits + offset
    lined = lax.broadcasted_iota(jnp.int32, logits.shape, 0)
    column = lax.broadcasted_iota(jnp.int32, logits.shape, 1)
    target = jnp.where(jnp.logical_and(m == place, lined == column), 1.0, 0.0)
    weights = (temper * (jax.nn.sigmoid(logits) - target)).astype(jnp.bfloat16)

    def add(ref, which):
        rows = pl.ds(pl.multiple_of(which * 288, 16), 288)

        @pl.when(side == 0)
        def _():
            ref[...] += lax.dot_general(
                xo[0, rows, :], weights, (((1,), (1,)), ((), ())), preferred_element_type=jnp.float32
            )

        @pl.when(side == 1)
        def _():
            ref[...] += lax.dot_general(
                xc[0, rows, :], weights, (((1,), (1,)), ((), ())), preferred_element_type=jnp.float32
            )

    add(send, 1 - core)
    add(keep, core)


def grads(info, scalars, yo, yc, xo, xc):
    n, k, r = xo.shape
    whole = pl.BlockSpec((k, r), lambda m: (0, 0))
    one = pl.BlockSpec((1, k, r), lambda m: (m, 0, 0))
    out = pl.BlockSpec((k // 2, r), lambda m: (0, 0))
    smem = pl.BlockSpec(memory_space=pltpu.SMEM)
    return pl.pallas_call(
        grads_kernel,
        grid=(n,),
        in_specs=[smem, smem, whole, whole, one, one],
        out_specs=[out, out],
        out_shape=[jax.ShapeDtypeStruct((k // 2, r), jnp.float32)] * 2,
        scratch_shapes=[pltpu.VMEM((2, r, k), jnp.bfloat16)],
        compiler_params=pltpu.CompilerParams(vmem_limit_bytes=32 * 2**20),
        cost_estimate=pl.CostEstimate(
            flops=n * 2 * r * r * k * 3, bytes_accessed=n * k * r * 4, transcendentals=n * r * r
        ),
    )(info, scalars, yo, yc, xo, xc)


def on_device(image_embed, text_embed, logit_scale, logit_bias):
    place = lax.axis_index("x")
    row = lax.axis_index("zl")
    core = lax.axis_index("core")
    text = lax.all_gather(text_embed.T, "core", axis=0, tiled=True)
    image = lax.all_gather(image_embed.T, "core", axis=0, tiled=True)
    x_own = jnp.where(core == 0, text, image)
    y_own = jnp.where(core == 0, image, text)
    x_far = flip(x_own)
    slots = jnp.arange(NX)[:, None, None]
    from_next = jnp.where(core == 0, slots < place, slots > place)

    def exchange(block):
        moved = shift_row(block)
        return lax.all_to_all(jnp.where(from_next, moved, block), "x", 0, 0, tiled=True)

    xo = exchange(x_own)
    y_far = swap_cores(x_far)
    xc = exchange(x_far)
    info = jnp.stack([place, row, core]).astype(jnp.int32)
    scalars = jnp.concatenate([logit_scale, logit_bias])
    keep, send = grads(info, scalars, y_own, y_far, xo, xc)
    got = swap_cores(send)
    image_grad = jnp.where(core == 0, keep, got)
    text_grad = jnp.where(core == 0, got, keep)
    return (image_grad.T, text_grad.T)


def solution(mesh):
    split = Mesh(mesh.devices.reshape(SIZES), AXES)
    block = P(("y", "zl", "x"), ("zh", "core"))
    return jax.shard_map(
        on_device, mesh=split, in_specs=(block, block, P(), P()), out_specs=(block, block), check_vma=False
    )
```

time: 320 us -> 130 us (0.41)
  the two profiles are of different devices: /device:TPU:1 before, /device:TPU:41 now
where the time goes in v1:
time: 130 us; the launch traced here: 129 us
  starting transfers between devices  46.1 us (35%)
  waiting for transfers between devices  37.9 us (29%)
  blocking collectives  31.8 us (24%)
  Pallas kernels  7 us (5%)
  other arithmetic  3.64 us (3%)
  between operations  2.01 us (2%)
    all_to_all x1, blocking collectives, exchange(): lax.all_to_all(jnp.where(from_next, moved, block), 'x', 0, 0, tiled=True)  26.8 us
    ppermute x2, starting transfers between devices, shift_row(): return lax.ppermute(block, AXES, route(next_row))  21.5 us
    all_to_all x1, waiting for transfers between devices, exchange(): lax.all_to_all(jnp.where(from_next, moved, block), 'x', 0, 0, tiled=True)  17.6 us
    ppermute x1, starting transfers between devices, flip(): lax.ppermute(block, AXES, route(lambda y, zl, x, zh, c: (y, zl, x, 1 - zh...  14.8 us
    ppermute x2, waiting for transfers between devices, shift_row(): return lax.ppermute(block, AXES, route(next_row))  10.2 us
    ppermute x1, waiting for transfers between devices, flip(): lax.ppermute(block, AXES, route(lambda y, zl, x, zh, c: (y, zl, x, 1 - zh...  8.38 us
    pallas_call x1, Pallas kernels, grads(): pl.pallas_call(grads_kernel, grid=(n,), in_specs=[smem, smem, whole, whol...  7 us
    ppermute x2, starting transfers between devices, swap_cores(): lax.ppermute(block, AXES, route(lambda y, zl, x, zh, c: (y, zl, x, zh, 1...  6.24 us
  transfers between devices with their start and end apart: 6, of which 6 were waited for; matrix products, arithmetic and copies ran while one was open for 0% of the time, Pallas kernels for 0%

profile of v1, /device:TPU:41, one launch (start us, length us, event | category | flops | bytes accessed | tf_op | source)
XLA Modules:
  0.0 129.5 jit_solution(5284553889275632567)
XLA Ops:
  0.6 2.6 %all_gather.6 = bf16[576,384]{1,0:T(8,128)(2,1)S(1)} all-gather(bf16[288,384]{1,0:T(8,128)(2,1)} %bitcast.9), channel_id=1, replica_groups=mesh['y'=8,'zl'=6,'x'=4,'zh'=2,'core'=2] {'core'}, dimensions={0}, use_global_device_ids=true | all-gather | bytes 663552 | tf_op jit(solution)/shard_map/all_gather | solution.py:109
  3.3 2.3 %all_gather.7 = bf16[576,384]{1,0:T(8,128)(2,1)S(1)} all-gather(bf16[288,384]{1,0:T(8,128)(2,1)} %bitcast.10), channel_id=1, replica_groups=mesh['y'=8,'zl'=6,'x'=4,'zh'=2,'core'=2] {'core'}, dimensions={0}, use_global_device_ids=true | all-gather | bytes 663552 | tf_op jit(solution)/shard_map/all_gather | solution.py:108
  5.6 0.8 broadcast_select_fusion.2
  6.4 14.8 %collective-permute-start = (bf16[576,384]{1,0:T(8,128)(2,1)S(1)}, bf16[576,384]{1,0:T(8,128)(2,1)S(1)}, u32[]{:S(2)}, u32[]{:S(2)}) collective-permute-start(bf16[576,384]{1,0:T(8,128)(2,1)S(1)} %get-tuple-element.8), channel_id=1, source_target_pairs={{0,2},{1,3},{2,0},{3,1},{4,6},{5,7},{6,4},{7,5},{8,10},{9,11},{10,... | collective-permute-start | bytes 1327112 | tf_op jit(solution)/shard_map/ppermute | solution.py:23
  21.3 2.7 %collective-permute-start.2 = (bf16[576,384]{1,0:T(8,128)(2,1)S(1)}, bf16[576,384]{1,0:T(8,128)(2,1)S(1)}, u32[]{:S(2)}, u32[]{:S(2)}) collective-permute-start(bf16[576,384]{1,0:T(8,128)(2,1)S(1)} %get-tuple-element.8), channel_id=1, source_target_pairs={{0,16},{1,755},{2,18},{3,753},{4,20},{5,759},{6,22},{7,757},{8,24}... | collective-permute-start | bytes 1327112 | tf_op jit(solution)/shard_map/ppermute | solution.py:39
  24.0 8.4 %collective-permute-done = bf16[576,384]{1,0:T(8,128)(2,1)S(1)} collective-permute-done((bf16[576,384]{1,0:T(8,128)(2,1)S(1)}, bf16[576,384]{1,0:T(8,128)(2,1)S(1)}, u32[]{:S(2)}, u32[]{:S(2)}) %collective-permute-start) | collective-permute-done | bytes 442400 | tf_op jit(solution)/shard_map/ppermute | solution.py:23
  32.4 0.0 copy-start.1
  32.4 18.8 %collective-permute-start.3 = (bf16[576,384]{1,0:T(8,128)(2,1)S(1)}, bf16[576,384]{1,0:T(8,128)(2,1)S(1)}, u32[]{:S(2)}, u32[]{:S(2)}) collective-permute-start(bf16[576,384]{1,0:T(8,128)(2,1)S(1)} %collective-permute-done), channel_id=1, source_target_pairs={{0,16},{1,755},{2,18},{3,753},{4,20},{5,759},{6,22},{7,757},{8,24}... | collective-permute-start | bytes 1327112 | tf_op jit(solution)/shard_map/ppermute | solution.py:39
  51.2 5.7 %collective-permute-done.2 = bf16[576,384]{1,0:T(8,128)(2,1)S(1)} collective-permute-done((bf16[576,384]{1,0:T(8,128)(2,1)S(1)}, bf16[576,384]{1,0:T(8,128)(2,1)S(1)}, u32[]{:S(2)}, u32[]{:S(2)}) %collective-permute-start.2) | collective-permute-done | bytes 442400 | tf_op jit(solution)/shard_map/ppermute | solution.py:39
  56.9 4.4 %collective-permute-done.3 = bf16[576,384]{1,0:T(8,128)(2,1)S(1)} collective-permute-done((bf16[576,384]{1,0:T(8,128)(2,1)S(1)}, bf16[576,384]{1,0:T(8,128)(2,1)S(1)}, u32[]{:S(2)}, u32[]{:S(2)}) %collective-permute-start.3) | collective-permute-done | bytes 442400 | tf_op jit(solution)/shard_map/ppermute | solution.py:39
  61.4 1.7 %broadcast_select_fusion = (bf16[4,576,384]{2,1,0:T(8,128)(2,1)S(1)}, bf16[4,576,384]{2,1,0:T(8,128)(2,1)}) fusion(pred[4]{0:T(512)(128)(4,1)S(1)} %compare_select_fusion, bf16[576,384]{1,0:T(8,128)(2,1)S(1)} %collective-permute-done, bf16[576,384]{1,0:T(8,128)(2,1)S(1)} %collective-permute-done.3, bf16[576,384]{1,0:T(8,128)(2,1)S(1)} %get-tuple-element.8, ...), kind=kLoop, calls=%fused_computation | loop fusion | flops 1769472 | bytes 5308420 | tf_op jit(solution)/shard_map/jit(_where)/select_n | solution.py:118
  63.0 0.0 copy-done.1
  63.1 26.8 %all_to_all.10.xc = bf16[4,576,384]{2,1,0:T(8,128)(2,1)S(1)} all-to-all(bf16[4,576,384]{2,1,0:T(8,128)(2,1)S(1)} %get-tuple-element.10), channel_id=1, replica_groups=mesh['y'=8,'zl'=6,'x'=4,'zh'=2,'core'=2] {'x'}, dimensions={0} | all-to-all | bytes 3538944 | tf_op jit(solution)/shard_map/all_to_all | solution.py:118
  89.8 3.6 %all-to-all-start = ((bf16[4,576,384]{2,1,0:T(8,128)(2,1)}), bf16[4,576,384]{2,1,0:T(8,128)(2,1)S(1)}, u32[]{:S(2)}, u32[]{:S(2)}) async-start(bf16[4,576,384]{2,1,0:T(8,128)(2,1)} %get-tuple-element.11), calls=%async_computation | async-start | bytes 3538944 | tf_op jit(solution)/shard_map/all_to_all | solution.py:118
  93.4 2.7 %collective-permute-start.1 = (bf16[576,384]{1,0:T(8,128)(2,1)}, bf16[576,384]{1,0:T(8,128)(2,1)}, u32[]{:S(2)}, u32[]{:S(2)}) collective-permute-start(bf16[576,384]{1,0:T(8,128)(2,1)} %copy-done.1), channel_id=1, source_target_pairs={{0,1},{1,0},{2,3},{3,2},{4,5},{5,4},{6,7},{7,6},{8,9},{9,8},{10,11... | collective-permute-start | bytes 1327112 | tf_op jit(solution)/shard_map/ppermute | solution.py:27
  97.4 0.1 pad_maximum_fusion.scalars
  97.5 0.1 pad_add_fusion.info
  97.6 0.3 collective-permute-done.1.yc
  97.9 17.6 %all-to-all-done.xo = bf16[4,576,384]{2,1,0:T(8,128)(2,1)S(1)} async-done(((bf16[4,576,384]{2,1,0:T(8,128)(2,1)}), bf16[4,576,384]{2,1,0:T(8,128)(2,1)S(1)}, u32[]{:S(2)}, u32[]{:S(2)}) %all-to-all-start) | async-done | bytes 1769504 | tf_op jit(solution)/shard_map/all_to_all | solution.py:118
  115.5 0.0 copy-start
  115.5 1.0 copy-done
  116.5 7.0 %shard_map.59 = (f32[288,384]{1,0:T(8,128)S(1)}, f32[288,384]{1,0:T(8,128)S(1)}) custom-call(s32[3]{0:T(128)S(1)} %pad_add_fusion.info, f32[2]{0:T(128)S(1)} %pad_maximum_fusion.scalars, bf16[576,384]{1,0:T(8,128)(2,1)S(1)} %copy-done, bf16[576,384]{1,0:T(8,128)(2,1)} %collective-permute-done.1.yc, bf16[4,576,384]{2,1,0:T(8,128)(2,1)S(1)} %all-to-all-done.xo, ...), custom_call_target="tpu_custom_call" | custom-call | flops 2038431744 | bytes 3538944 | tf_op jit(solution)/shard_map/pallas_call | solution.py:90
  123.5 3.6 %collective-permute-start.4 = (f32[288,384]{1,0:T(8,128)S(1)}, f32[288,384]{1,0:T(8,128)S(1)}, u32[]{:S(2)}, u32[]{:S(2)}) collective-permute-start(f32[288,384]{1,0:T(8,128)S(1)} %get-tuple-element.5), channel_id=1, source_target_pairs={{0,1},{1,0},{2,3},{3,2},{4,5},{5,4},{6,7},{7,6},{8,9},{9,8},{10,11... | collective-permute-start | bytes 1327112 | tf_op jit(solution)/shard_map/ppermute | solution.py:27
  127.1 1.4 %collective-permute-done.4 = f32[288,384]{1,0:T(8,128)S(1)} collective-permute-done((f32[288,384]{1,0:T(8,128)S(1)}, f32[288,384]{1,0:T(8,128)S(1)}, u32[]{:S(2)}, u32[]{:S(2)}) %collective-permute-start.4) | collective-permute-done | bytes 442400 | tf_op jit(solution)/shard_map/ppermute | solution.py:27
  128.5 1.0 select_bitcast_fusion
  (1 shorter events, 0.0 us)
Async XLA Ops:
  6.4 25.9 %collective-permute-start = (bf16[576,384]{1,0:T(8,128)(2,1)S(1)}, bf16[576,384]{1,0:T(8,128)(2,1)S(1)}, u32[]{:S(2)}, u32[]{:S(2)}) collective-permute-start(bf16[576,384]{1,0:T(8,128)(2,1)S(1)} %get-tuple-element.8), channel_id=1, source_target_pairs={{0,2},{1,3},{2,0},{3,1},{4,6},{5,7},{6,4},{7,5},{8,10},{9,11},{10,... | collective-permute-start | bytes 1327112 | tf_op jit(solution)/shard_map/ppermute | solution.py:23
  21.3 35.6 %collective-permute-start.2 = (bf16[576,384]{1,0:T(8,128)(2,1)S(1)}, bf16[576,384]{1,0:T(8,128)(2,1)S(1)}, u32[]{:S(2)}, u32[]{:S(2)}) collective-permute-start(bf16[576,384]{1,0:T(8,128)(2,1)S(1)} %get-tuple-element.8), channel_id=1, source_target_pairs={{0,16},{1,755},{2,18},{3,753},{4,20},{5,759},{6,22},{7,757},{8,24}... | collective-permute-start | bytes 1327112 | tf_op jit(solution)/shard_map/ppermute | solution.py:39
  32.4 30.7 %copy-start.1 = (bf16[576,384]{1,0:T(8,128)(2,1)}, bf16[576,384]{1,0:T(8,128)(2,1)S(1)}, u32[]{:S(2)}) copy-start(bf16[576,384]{1,0:T(8,128)(2,1)S(1)} %collective-permute-done) | copy-start | bytes 1327108
  32.4 29.0 %collective-permute-start.3 = (bf16[576,384]{1,0:T(8,128)(2,1)S(1)}, bf16[576,384]{1,0:T(8,128)(2,1)S(1)}, u32[]{:S(2)}, u32[]{:S(2)}) collective-permute-start(bf16[576,384]{1,0:T(8,128)(2,1)S(1)} %collective-permute-done), channel_id=1, source_target_pairs={{0,16},{1,755},{2,18},{3,753},{4,20},{5,759},{6,22},{7,757},{8,24}... | collective-permute-start | bytes 1327112 | tf_op jit(solution)/shard_map/ppermute | solution.py:39
  89.8 25.7 %all-to-all-start = ((bf16[4,576,384]{2,1,0:T(8,128)(2,1)}), bf16[4,576,384]{2,1,0:T(8,128)(2,1)S(1)}, u32[]{:S(2)}, u32[]{:S(2)}) async-start(bf16[4,576,384]{2,1,0:T(8,128)(2,1)} %get-tuple-element.11), calls=%async_computation | async-start | bytes 3538944 | tf_op jit(solution)/shard_map/all_to_all | solution.py:118
  93.4 4.4 %collective-permute-start.1 = (bf16[576,384]{1,0:T(8,128)(2,1)}, bf16[576,384]{1,0:T(8,128)(2,1)}, u32[]{:S(2)}, u32[]{:S(2)}) collective-permute-start(bf16[576,384]{1,0:T(8,128)(2,1)} %copy-done.1), channel_id=1, source_target_pairs={{0,1},{1,0},{2,3},{3,2},{4,5},{5,4},{6,7},{7,6},{8,9},{9,8},{10,11... | collective-permute-start | bytes 1327112 | tf_op jit(solution)/shard_map/ppermute | solution.py:27
  115.5 1.0 copy-start
  123.5 5.0 %collective-permute-start.4 = (f32[288,384]{1,0:T(8,128)S(1)}, f32[288,384]{1,0:T(8,128)S(1)}, u32[]{:S(2)}, u32[]{:S(2)}) collective-permute-start(f32[288,384]{1,0:T(8,128)S(1)} %get-tuple-element.5), channel_id=1, source_target_pairs={{0,1},{1,0},{2,3},{3,2},{4,5},{5,4},{6,7},{7,6},{8,9},{9,8},{10,11... | collective-permute-start | bytes 1327112 | tf_op jit(solution)/shard_map/ppermute | solution.py:27

commit v2 on v0

v2 whole, which is shorter than its diff:
```python
import numpy as np
import jax
import jax.numpy as jnp
from jax import lax
from jax.experimental import pallas as pl
from jax.experimental.pallas import tpu as pltpu
from jax.sharding import Mesh, PartitionSpec as P

AXES = ("y", "zl", "x", "zh", "core")
SIZES = (8, 6, 4, 2, 2)
NX = 4
STEPS = 4
F32 = jnp.float32
BF16 = jnp.bfloat16
HERE = pl.BlockSpec(memory_space=pltpu.VMEM)
SMEM = pl.BlockSpec(memory_space=pltpu.SMEM)


def send(block, move):
    pairs = []
    for i, place in enumerate(np.ndindex(*SIZES)):
        goal = [a % b for a, b in zip(move(*place), SIZES)]
        pairs.append((i, int(np.ravel_multi_index(goal, SIZES))))
    return lax.ppermute(block, AXES, pairs)


def flip(block):
    return send(block, lambda y, zl, x, zh, c: (y, zl, x, 1 - zh, c))


def swap_cores(block):
    return send(block, lambda y, zl, x, zh, c: (y, zl, x, zh, 1 - c))


def next_row(y, zl, x, zh, c):
    step = 1 if c == 0 else -1
    z = (zh * 6 + zl + step) % 12
    row = zl + step
    y = y + 1 if row > 5 else y - 1 if row < 0 else y
    return (y, z % 6, x, z // 6, c)


def along_dp(block, s):
    def move(y, zl, x, zh, c):
        to = x + s if c == 0 else x - s
        if not 0 <= to < NX:
            y, zl, x, zh, c = next_row(y, zl, x, zh, c)
        return (y, zl, to, zh, c)

    return send(block, move)


def call(kernel, args, out_shape, flops, moved, scratch=()):
    n = len(out_shape)
    return pl.pallas_call(
        kernel,
        in_specs=[SMEM, SMEM] + [HERE] * (len(args) - 2),
        out_specs=[HERE] * n,
        out_shape=out_shape,
        scratch_shapes=scratch,
        compiler_params=pltpu.CompilerParams(vmem_limit_bytes=40 * 2**20),
        cost_estimate=pl.CostEstimate(flops=flops, bytes_accessed=moved, transcendentals=0),
    )(*args)


def near_kernel(info, scalars, ya, yb, xa, xb, x1, x2, x3, logits, yt):
    k = ya.shape[0]
    yt[0], yt[1] = ya[...].T, yb[...].T
    logits[0] = dot(yt[0], xa[...]) + dot(yt[1], xb[...])
    for m, x in enumerate((x1, x2, x3), 1):

        @pl.when(info[m] == 0)
        def _():
            logits[m] = dot(yt[0], x[0:k]) + dot(yt[1], x[k : 2 * k])


def dot(a, b):
    return jnp.dot(a, b, preferred_element_type=F32)


def add_to(total, x, weights):
    total[...] += lax.dot_general(x, weights, (((1,), (1,)), ((), ())), preferred_element_type=F32)


def weights_kernel(info, scalars, near, yt, yc, xb, x1, x2, x3, *refs):
    far, (weights, total, yct, logits) = refs[:4], refs[4:]
    temper, offset = scalars[0], scalars[1]
    k, r = xb.shape
    total[...] = jnp.zeros_like(total)
    yct[0], yct[1] = yc[k : 2 * k].T, yc[0:k].T
    for m in range(STEPS):
        near_x = (None, x1, x2, x3)[m]
        far_x = far[m]
        if m == 0:
            logits[...] = near[m] + (dot(yct[0], far_x[0:k]) + dot(yct[1], far_x[k : 2 * k]))
        else:

            @pl.when(info[m] == 0)
            def _():
                logits[...] = near[m] + (dot(yct[0], far_x[0:k]) + dot(yct[1], far_x[k : 2 * k]))

            @pl.when(info[m] == 1)
            def _():
                logits[...] = (dot(yct[0], near_x[0:k]) + dot(yct[1], near_x[k : 2 * k])) + (
                    dot(yt[0], far_x[0:k]) + dot(yt[1], far_x[k : 2 * k])
                )

        value = jax.nn.sigmoid(temper * logits[...] + offset)
        if m == 0:
            lined = lax.broadcasted_iota(jnp.int32, (r, r), 0)
            column = lax.broadcasted_iota(jnp.int32, (r, r), 1)
            value = value - jnp.where(lined == column, 1.0, 0.0)
        weights[m] = (temper * value).astype(BF16)
        if m == 0:
            add_to(total, xb[...], weights[m])
        else:

            @pl.when(info[m] == 0)
            def _():
                add_to(total, near_x[k : 2 * k], weights[m])

            @pl.when(info[m] == 1)
            def _():
                add_to(total, far_x[k : 2 * k], weights[m])


def keep_kernel(info, scalars, weights, xa, x1, x2, x3, xc1, xc2, xc3, total):
    k, r = xa.shape
    total[...] = jnp.zeros_like(total)
    add_to(total, xa[...], weights[0])
    for m, (near_x, far_x) in enumerate(((x1, xc1), (x2, xc2), (x3, xc3)), 1):

        @pl.when(info[m] == 0)
        def _():
            add_to(total, near_x[0:k], weights[m])

        @pl.when(info[m] == 1)
        def _():
            add_to(total, far_x[0:k], weights[m])


def on_device(image_embed, text_embed, logit_scale, logit_bias):
    place = lax.axis_index("x")
    row = lax.axis_index("zl")
    core = lax.axis_index("core")
    text, image = text_embed.T, image_embed.T
    k, r = text.shape
    xa = jnp.where(core == 0, text, image)
    ya = jnp.where(core == 0, image, text)
    with jax.named_scope("cross_a"):
        xca = flip(xa)
    with jax.named_scope("share"):
        other = swap_cores(jnp.concatenate([ya, xa], axis=0))
    xb, yb = other[:k], other[k:]
    with jax.named_scope("cross_b"):
        xcb = flip(xb)
    own = jnp.concatenate([xa, xb], axis=0)
    near_x = []
    for s in range(1, STEPS):
        with jax.named_scope("near"):
            near_x.append(along_dp(own, s))
    xc = jnp.concatenate([xca, xcb], axis=0)
    far_x = [xc]
    for s in range(1, STEPS):
        with jax.named_scope("far"):
            far_x.append(along_dp(xc, s))
    with jax.named_scope("share_far"):
        yc = swap_cores(xc)

    came = [jnp.where(core == 0, place - s < 0, place + s >= NX) for s in range(STEPS)]
    edge = jnp.where(core == 0, row == 0, row == 5)
    info = jnp.stack([jnp.logical_and(c, edge) for c in came]).astype(jnp.int32)
    scalars = jnp.concatenate([logit_scale, logit_bias])
    logits = jax.ShapeDtypeStruct((STEPS, r, r), F32)
    work = 2 * STEPS * k * r * r
    near, yt = call(
        near_kernel,
        (info, scalars, ya, yb, xa, xb, *near_x),
        [logits, jax.ShapeDtypeStruct((2, r, k), BF16)],
        2 * work,
        STEPS * r * (4 * r + 4 * k),
    )
    weights, total = call(
        weights_kernel,
        (info, scalars, near, yt, yc, xb, *near_x, *far_x),
        [jax.ShapeDtypeStruct((STEPS, r, r), BF16), jax.ShapeDtypeStruct((k, r), F32)],
        3 * work,
        STEPS * r * (8 * r + 8 * k),
        [pltpu.VMEM((2, r, k), BF16), pltpu.VMEM((r, r), F32)],
    )
    with jax.named_scope("give"):
        got = swap_cores(total)
    (keep,) = call(
        keep_kernel,
        (info, scalars, weights, xa, *near_x, *far_x[1:]),
        [jax.ShapeDtypeStruct((k, r), F32)],
        work,
        STEPS * r * (2 * r + 4 * k),
    )
    image_grad = jnp.where(core == 0, keep, got)
    text_grad = jnp.where(core == 0, got, keep)
    return (image_grad.T, text_grad.T)


def solution(mesh):
    split = Mesh(mesh.devices.reshape(SIZES), AXES)
    block = P(("y", "zl", "x"), ("zh", "core"))
    return jax.shard_map(
        on_device, mesh=split, in_specs=(block, block, P(), P()), out_specs=(block, block), check_vma=False
    )
```

time: 320 us -> 97.2 us (0.30); the launches traced: 314 us -> 96.7 us
  waiting for transfers between devices: 270 us -> 10.6 us
  starting transfers between devices: 16.9 us -> 68.9 us
  between operations: 15.5 us -> 2.18 us
  matrix products: 9.51 us -> 0 us
  Pallas kernels: 0 us -> 9.17 us
    psum x1 -> x0, waiting for transfers between devices: 166 us -> none  [loss_weights(): logits = temper * lax.psum(partial_value, 'width') + offset]
    ppermute x7 -> x11, waiting for transfers between devices: 104 us -> 10.6 us  [send(): return lax.ppermute(block, AXES, pairs)]
    ppermute x7 -> x11, starting transfers between devices: 16.9 us -> 68.9 us  [send(): return lax.ppermute(block, AXES, pairs)]
    dot_general x12 -> x0, matrix products: 9.51 us -> none  [the longest x4 5.71 us: on_device(): lax.dot_general(image_embed, text_rows, (((1,), (1,)), ((), ())), preferr...]
    pallas_call x0 -> x3, Pallas kernels: none -> 9.17 us  [call(): pl.pallas_call(kernel, in_specs=[SMEM, SMEM] + [HERE] * (len(args) - 2),...]
  transfers between devices with their start and end apart: 8 -> 11, of which waited for: 8 -> 2; matrix products, arithmetic and copies ran while one was open for 2% -> 2% of each run, Pallas kernels for 0% -> 5%
where the time goes in v2:
time: 97.2 us; the launch traced here: 96.7 us
  starting transfers between devices  68.9 us (71%)
  waiting for transfers between devices  10.6 us (11%)
  Pallas kernels  9.17 us (9%)
  other arithmetic  3.07 us (3%)
  local copies, waits for them, and re-layouts  2.67 us (3%)
  between operations  2.18 us (2%)
    ppermute x11, starting transfers between devices, send(): return lax.ppermute(block, AXES, pairs)  68.9 us
    ppermute x11, waiting for transfers between devices, send(): return lax.ppermute(block, AXES, pairs)  10.6 us
    pallas_call x3, Pallas kernels, call(): pl.pallas_call(kernel, in_specs=[SMEM, SMEM] + [HERE] * (len(args) - 2),...  9.17 us
  transfers between devices with their start and end apart: 11, of which 2 were waited for; matrix products, arithmetic and copies ran while one was open for 2% of the time, Pallas kernels for 5%

profile of v2, /device:TPU:1, one launch (start us, length us, event | category | flops | bytes accessed | tf_op | source)
XLA Modules:
  0.0 96.7 jit_solution(10985121471779194898)
XLA Ops:
  0.6 1.1 %select_bitcast_fusion.2 = (bf16[288,384]{1,0:T(8,128)(2,1)S(1)}, bf16[288,384]{1,0:T(8,128)(2,1)S(1)}) fusion(bf16[384,288]{0,1:T(8,128)(2,1)} %param.5, bf16[384,288]{0,1:T(8,128)(2,1)} %param.4, pred[]{:T(512)S(6)} %eq.6), kind=kLoop, calls=%fused_computation.4 | loop fusion | flops 221184 | bytes 884737 | tf_op jit(solution)/shard_map/jit(_where)/select_n | solution.py:148
  1.7 0.0 copy-start
  1.8 12.4 %collective-permute-start = (bf16[576,384]{1,0:T(8,128)(2,1)S(1)}, bf16[576,384]{1,0:T(8,128)(2,1)S(1)}, u32[]{:S(2)}, u32[]{:S(2)}) collective-permute-start(bf16[576,384]{1,0:T(8,128)(2,1)S(1)} %pad_maximum_fusion), channel_id=1, source_target_pairs={{0,1},{1,0},{2,3},{3,2},{4,5},{5,4},{6,7},{7,6},{8,9},{9,8},{10,11... | collective-permute-start | bytes 1327112 | tf_op jit(solution)/shard_map/share/ppermute | solution.py:24
  14.2 5.8 %collective-permute-start.4 = (bf16[288,384]{1,0:T(8,128)(2,1)S(1)}, bf16[288,384]{1,0:T(8,128)(2,1)S(1)}, u32[]{:S(2)}, u32[]{:S(2)}) collective-permute-start(bf16[288,384]{1,0:T(8,128)(2,1)S(1)} %get-tuple-element.14.xa), channel_id=1, source_target_pairs={{0,2},{1,3},{2,0},{3,1},{4,6},{5,7},{6,4},{7,5},{8,10},{9,11},{10,... | collective-permute-start | bytes 663560 | tf_op jit(solution)/shard_map/cross_a/ppermute | solution.py:24
  20.1 0.7 fusion
  20.8 0.8 pad_maximum_fusion.1
  21.6 5.7 %collective-permute-start.3 = (bf16[576,384]{1,0:T(8,128)(2,1)}, bf16[576,384]{1,0:T(8,128)(2,1)S(1)}, u32[]{:S(2)}, u32[]{:S(2)}) collective-permute-start(bf16[576,384]{1,0:T(8,128)(2,1)} %pad_maximum_fusion.1), channel_id=1, source_target_pairs={{0,12},{1,759},{2,14},{3,757},{4,16},{5,763},{6,18},{7,761},{8,20}... | collective-permute-start | bytes 1327112 | tf_op jit(solution)/shard_map/near/ppermute | solution.py:24
  27.3 3.8 %collective-permute-start.2 = (bf16[576,384]{1,0:T(8,128)(2,1)}, bf16[576,384]{1,0:T(8,128)(2,1)S(1)}, u32[]{:S(2)}, u32[]{:S(2)}) collective-permute-start(bf16[576,384]{1,0:T(8,128)(2,1)} %pad_maximum_fusion.1), channel_id=1, source_target_pairs={{0,8},{1,763},{2,10},{3,761},{4,12},{5,767},{6,14},{7,765},{8,16},... | collective-permute-start | bytes 1327112 | tf_op jit(solution)/shard_map/near/ppermute | solution.py:24
  31.2 9.7 %collective-permute-start.5 = (bf16[288,384]{1,0:T(8,128)(2,1)S(1)}, bf16[288,384]{1,0:T(8,128)(2,1)S(1)}, u32[]{:S(2)}, u32[]{:S(2)}) collective-permute-start(bf16[288,384]{1,0:T(8,128)(2,1)S(1)} %get-tuple-element.12.xb), channel_id=1, source_target_pairs={{0,2},{1,3},{2,0},{3,1},{4,6},{5,7},{6,4},{7,5},{8,10},{9,11},{10,... | collective-permute-start | bytes 663560 | tf_op jit(solution)/shard_map/cross_b/ppermute | solution.py:24
  40.9 0.0 collective-permute-done.4
  40.9 4.1 %collective-permute-start.1 = (bf16[576,384]{1,0:T(8,128)(2,1)}, bf16[576,384]{1,0:T(8,128)(2,1)S(1)}, u32[]{:S(2)}, u32[]{:S(2)}) collective-permute-start(bf16[576,384]{1,0:T(8,128)(2,1)} %pad_maximum_fusion.1), channel_id=1, source_target_pairs={{0,4},{1,767},{2,6},{3,765},{4,8},{5,1},{6,10},{7,3},{8,12},{9,5},... | collective-permute-start | bytes 1327112 | tf_op jit(solution)/shard_map/near/ppermute | solution.py:24
  45.0 7.0 %collective-permute-done.5 = bf16[288,384]{1,0:T(8,128)(2,1)S(1)} collective-permute-done((bf16[288,384]{1,0:T(8,128)(2,1)S(1)}, bf16[288,384]{1,0:T(8,128)(2,1)S(1)}, u32[]{:S(2)}, u32[]{:S(2)}) %collective-permute-start.5) | collective-permute-done | bytes 221216 | tf_op jit(solution)/shard_map/cross_b/ppermute | solution.py:24
  52.0 16.5 %collective-permute-start.9 = (bf16[576,384]{1,0:T(8,128)(2,1)S(1)}, bf16[576,384]{1,0:T(8,128)(2,1)S(1)}, u32[]{:S(2)}, u32[]{:S(2)}) collective-permute-start(bf16[576,384]{1,0:T(8,128)(2,1)S(1)} %constant_dynamic-update-slice_fusion.refs_0_), channel_id=1, source_target_pairs={{0,12},{1,759},{2,14},{3,757},{4,16},{5,763},{6,18},{7,761},{8,20}... | collective-permute-start | bytes 1327112 | tf_op jit(solution)/shard_map/far/ppermute | solution.py:24
  68.5 1.9 %collective-permute-start.8 = (bf16[576,384]{1,0:T(8,128)(2,1)S(1)}, bf16[576,384]{1,0:T(8,128)(2,1)S(1)}, u32[]{:S(2)}, u32[]{:S(2)}) collective-permute-start(bf16[576,384]{1,0:T(8,128)(2,1)S(1)} %constant_dynamic-update-slice_fusion.refs_0_), channel_id=1, source_target_pairs={{0,8},{1,763},{2,10},{3,761},{4,12},{5,767},{6,14},{7,765},{8,16},... | collective-permute-start | bytes 1327112 | tf_op jit(solution)/shard_map/far/ppermute | solution.py:24
  70.4 0.0 collective-permute-done.3.x3
  70.4 4.3 %collective-permute-start.7 = (bf16[576,384]{1,0:T(8,128)(2,1)S(1)}, bf16[576,384]{1,0:T(8,128)(2,1)S(1)}, u32[]{:S(2)}, u32[]{:S(2)}) collective-permute-start(bf16[576,384]{1,0:T(8,128)(2,1)S(1)} %constant_dynamic-update-slice_fusion.refs_0_), channel_id=1, source_target_pairs={{0,4},{1,767},{2,6},{3,765},{4,8},{5,1},{6,10},{7,3},{8,12},{9,5},... | collective-permute-start | bytes 1327112 | tf_op jit(solution)/shard_map/far/ppermute | solution.py:24
  74.8 1.9 %collective-permute-start.6 = (bf16[576,384]{1,0:T(8,128)(2,1)S(1)}, bf16[576,384]{1,0:T(8,128)(2,1)}, u32[]{:S(2)}, u32[]{:S(2)}) collective-permute-start(bf16[576,384]{1,0:T(8,128)(2,1)S(1)} %constant_dynamic-update-slice_fusion.refs_0_), channel_id=1, source_target_pairs={{0,1},{1,0},{2,3},{3,2},{4,5},{5,4},{6,7},{7,6},{8,9},{9,8},{10,11... | collective-permute-start | bytes 1327112 | tf_op jit(solution)/shard_map/share_far/ppermute | solution.py:24
  78.0 0.1 pad_maximum_fusion.2.scalars
  78.1 0.1 add_convert_fusion.info
  78.2 0.0 collective-permute-done.1.x1
  78.2 0.9 copy-done.1
  79.1 0.9 copy-done.2
  80.1 2.6 %shard_map.59 = (f32[4,384,384]{2,1,0:T(8,128)S(1)}, bf16[2,384,288]{2,1,0:T(8,128)(2,1)S(1)}) custom-call(s32[4]{0:T(128)S(1)} %add_convert_fusion.info, f32[2]{0:T(128)S(1)} %pad_maximum_fusion.2.scalars, bf16[288,384]{1,0:T(8,128)(2,1)S(1)} %copy-done.1, bf16[288,384]{1,0:T(8,128)(2,1)S(1)} %copy-done.2, bf16[288,384]{1,0:T(8,128)(2,1)S(1)} %get-tuple-element.14.xa, ...), custom_call_target="tpu_custom_call" | custom-call | flops 679477248 | bytes 4128768 | tf_op jit(solution)/shard_map/pallas_call | solution.py:55
  82.7 0.0 collective-permute-done.9.refs_3_.xc3
  82.7 3.6 %collective-permute-done.8.refs_2_.xc2 = bf16[576,384]{1,0:T(8,128)(2,1)S(1)} collective-permute-done((bf16[576,384]{1,0:T(8,128)(2,1)S(1)}, bf16[576,384]{1,0:T(8,128)(2,1)S(1)}, u32[]{:S(2)}, u32[]{:S(2)}) %collective-permute-start.8) | collective-permute-done | bytes 442400 | tf_op jit(solution)/shard_map/far/ppermute | solution.py:24
  86.4 0.0 collective-permute-done.7.refs_1_.xc1
  86.4 0.0 collective-permute-done.6.yc
  86.4 4.7 %shard_map.60 = (bf16[4,384,384]{2,1,0:T(8,128)(2,1)S(1)}, f32[288,384]{1,0:T(8,128)S(1)}) custom-call(s32[4]{0:T(128)S(1)} %add_convert_fusion.info, f32[2]{0:T(128)S(1)} %pad_maximum_fusion.2.scalars, f32[4,384,384]{2,1,0:T(8,128)S(1)} %get-tuple-element.6.near, bf16[2,384,288]{2,1,0:T(8,128)(2,1)S(1)} %get-tuple-element.7.yt, ...), custom_call_target="tpu_custom_call" | custom-call | flops 1019215872 | bytes 8257536 | tf_op jit(solution)/shard_map/pallas_call | solution.py:55
  91.1 2.7 %collective-permute-start.10 = (f32[288,384]{1,0:T(8,128)S(1)}, f32[288,384]{1,0:T(8,128)S(1)}, u32[]{:S(2)}, u32[]{:S(2)}) collective-permute-start(f32[288,384]{1,0:T(8,128)S(1)} %get-tuple-element.9), channel_id=1, source_target_pairs={{0,1},{1,0},{2,3},{3,2},{4,5},{5,4},{6,7},{7,6},{8,9},{9,8},{10,11... | collective-permute-start | bytes 1327112 | tf_op jit(solution)/shard_map/give/ppermute | solution.py:24
  93.9 1.8 %shard_map.61 = f32[288,384]{1,0:T(8,128)S(1)} custom-call(s32[4]{0:T(128)S(1)} %add_convert_fusion.info, f32[2]{0:T(128)S(1)} %pad_maximum_fusion.2.scalars, bf16[4,384,384]{2,1,0:T(8,128)(2,1)S(1)} %get-tuple-element.8.weights, bf16[288,384]{1,0:T(8,128)(2,1)S(1)} %get-tuple-element.14.xa, bf16[576,384]{1,0:T(8,128)(2,1)S(1)} %collective-permute-done.1.x1, ...), custom_call_target="tpu_custom_call" | custom-call | flops 339738624 | bytes 2949120 | tf_op jit(solution)/shard_map/pallas_call | solution.py:55
  95.7 0.0 collective-permute-done.10
  95.7 1.0 %select_bitcast_fusion = (f32[384,288]{0,1:T(8,128)}, f32[384,288]{0,1:T(8,128)}) fusion(f32[288,384]{1,0:T(8,128)S(1)} %collective-permute-done.10, f32[288,384]{1,0:T(8,128)S(1)} %shard_map.61, pred[]{:T(512)S(6)} %eq.6), kind=kLoop, calls=%fused_computation.2 | loop fusion | flops 221184 | bytes 1769473 | tf_op jit(solution)/shard_map/transpose | solution.py:202
  (8 shorter events, 0.1 us)
Async XLA Ops:
  1.7 73.0 %copy-start = (bf16[288,384]{1,0:T(8,128)(2,1)}, bf16[288,384]{1,0:T(8,128)(2,1)S(1)}, u32[]{:S(2)}) copy-start(bf16[288,384]{1,0:T(8,128)(2,1)S(1)} %get-tuple-element.15.ya) | copy-start | bytes 663556
  1.8 18.3 %collective-permute-start = (bf16[576,384]{1,0:T(8,128)(2,1)S(1)}, bf16[576,384]{1,0:T(8,128)(2,1)S(1)}, u32[]{:S(2)}, u32[]{:S(2)}) collective-permute-start(bf16[576,384]{1,0:T(8,128)(2,1)S(1)} %pad_maximum_fusion), channel_id=1, source_target_pairs={{0,1},{1,0},{2,3},{3,2},{4,5},{5,4},{6,7},{7,6},{8,9},{9,8},{10,11... | collective-permute-start | bytes 1327112 | tf_op jit(solution)/shard_map/share/ppermute | solution.py:24
  14.2 26.6 %collective-permute-start.4 = (bf16[288,384]{1,0:T(8,128)(2,1)S(1)}, bf16[288,384]{1,0:T(8,128)(2,1)S(1)}, u32[]{:S(2)}, u32[]{:S(2)}) collective-permute-start(bf16[288,384]{1,0:T(8,128)(2,1)S(1)} %get-tuple-element.14.xa), channel_id=1, source_target_pairs={{0,2},{1,3},{2,0},{3,1},{4,6},{5,7},{6,4},{7,5},{8,10},{9,11},{10,... | collective-permute-start | bytes 663560 | tf_op jit(solution)/shard_map/cross_a/ppermute | solution.py:24
  21.6 48.8 %collective-permute-start.3 = (bf16[576,384]{1,0:T(8,128)(2,1)}, bf16[576,384]{1,0:T(8,128)(2,1)S(1)}, u32[]{:S(2)}, u32[]{:S(2)}) collective-permute-start(bf16[576,384]{1,0:T(8,128)(2,1)} %pad_maximum_fusion.1), channel_id=1, source_target_pairs={{0,12},{1,759},{2,14},{3,757},{4,16},{5,763},{6,18},{7,761},{8,20}... | collective-permute-start | bytes 1327112 | tf_op jit(solution)/shard_map/near/ppermute | solution.py:24
  27.3 47.4 %collective-permute-start.2 = (bf16[576,384]{1,0:T(8,128)(2,1)}, bf16[576,384]{1,0:T(8,128)(2,1)S(1)}, u32[]{:S(2)}, u32[]{:S(2)}) collective-permute-start(bf16[576,384]{1,0:T(8,128)(2,1)} %pad_maximum_fusion.1), channel_id=1, source_target_pairs={{0,8},{1,763},{2,10},{3,761},{4,12},{5,767},{6,14},{7,765},{8,16},... | collective-permute-start | bytes 1327112 | tf_op jit(solution)/shard_map/near/ppermute | solution.py:24
  31.2 20.8 %collective-permute-start.5 = (bf16[288,384]{1,0:T(8,128)(2,1)S(1)}, bf16[288,384]{1,0:T(8,128)(2,1)S(1)}, u32[]{:S(2)}, u32[]{:S(2)}) collective-permute-start(bf16[288,384]{1,0:T(8,128)(2,1)S(1)} %get-tuple-element.12.xb), channel_id=1, source_target_pairs={{0,2},{1,3},{2,0},{3,1},{4,6},{5,7},{6,4},{7,5},{8,10},{9,11},{10,... | collective-permute-start | bytes 663560 | tf_op jit(solution)/shard_map/cross_b/ppermute | solution.py:24
  40.9 37.3 %collective-permute-start.1 = (bf16[576,384]{1,0:T(8,128)(2,1)}, bf16[576,384]{1,0:T(8,128)(2,1)S(1)}, u32[]{:S(2)}, u32[]{:S(2)}) collective-permute-start(bf16[576,384]{1,0:T(8,128)(2,1)} %pad_maximum_fusion.1), channel_id=1, source_target_pairs={{0,4},{1,767},{2,6},{3,765},{4,8},{5,1},{6,10},{7,3},{8,12},{9,5},... | collective-permute-start | bytes 1327112 | tf_op jit(solution)/shard_map/near/ppermute | solution.py:24
  52.0 30.7 %collective-permute-start.9 = (bf16[576,384]{1,0:T(8,128)(2,1)S(1)}, bf16[576,384]{1,0:T(8,128)(2,1)S(1)}, u32[]{:S(2)}, u32[]{:S(2)}) collective-permute-start(bf16[576,384]{1,0:T(8,128)(2,1)S(1)} %constant_dynamic-update-slice_fusion.refs_0_), channel_id=1, source_target_pairs={{0,12},{1,759},{2,14},{3,757},{4,16},{5,763},{6,18},{7,761},{8,20}... | collective-permute-start | bytes 1327112 | tf_op jit(solution)/shard_map/far/ppermute | solution.py:24
  68.5 17.9 %collective-permute-start.8 = (bf16[576,384]{1,0:T(8,128)(2,1)S(1)}, bf16[576,384]{1,0:T(8,128)(2,1)S(1)}, u32[]{:S(2)}, u32[]{:S(2)}) collective-permute-start(bf16[576,384]{1,0:T(8,128)(2,1)S(1)} %constant_dynamic-update-slice_fusion.refs_0_), channel_id=1, source_target_pairs={{0,8},{1,763},{2,10},{3,761},{4,12},{5,767},{6,14},{7,765},{8,16},... | collective-permute-start | bytes 1327112 | tf_op jit(solution)/shard_map/far/ppermute | solution.py:24
  70.4 15.9 %collective-permute-start.7 = (bf16[576,384]{1,0:T(8,128)(2,1)S(1)}, bf16[576,384]{1,0:T(8,128)(2,1)S(1)}, u32[]{:S(2)}, u32[]{:S(2)}) collective-permute-start(bf16[576,384]{1,0:T(8,128)(2,1)S(1)} %constant_dynamic-update-slice_fusion.refs_0_), channel_id=1, source_target_pairs={{0,4},{1,767},{2,6},{3,765},{4,8},{5,1},{6,10},{7,3},{8,12},{9,5},... | collective-permute-start | bytes 1327112 | tf_op jit(solution)/shard_map/far/ppermute | solution.py:24
  74.8 11.6 %collective-permute-start.6 = (bf16[576,384]{1,0:T(8,128)(2,1)S(1)}, bf16[576,384]{1,0:T(8,128)(2,1)}, u32[]{:S(2)}, u32[]{:S(2)}) collective-permute-start(bf16[576,384]{1,0:T(8,128)(2,1)S(1)} %constant_dynamic-update-slice_fusion.refs_0_), channel_id=1, source_target_pairs={{0,1},{1,0},{2,3},{3,2},{4,5},{5,4},{6,7},{7,6},{8,9},{9,8},{10,11... | collective-permute-start | bytes 1327112 | tf_op jit(solution)/shard_map/share_far/ppermute | solution.py:24
  78.2 0.9 copy-start.1
  79.1 0.9 copy-start.2
  91.1 4.5 %collective-permute-start.10 = (f32[288,384]{1,0:T(8,128)S(1)}, f32[288,384]{1,0:T(8,128)S(1)}, u32[]{:S(2)}, u32[]{:S(2)}) collective-permute-start(f32[288,384]{1,0:T(8,128)S(1)} %get-tuple-element.9), channel_id=1, source_target_pairs={{0,1},{1,0},{2,3},{3,2},{4,5},{5,4},{6,7},{7,6},{8,9},{9,8},{10,11... | collective-permute-start | bytes 1327112 | tf_op jit(solution)/shard_map/give/ppermute | solution.py:24

commit v3 on v2

v3 whole, which is shorter than its diff:
```python
import functools

import numpy as np
import jax
import jax.numpy as jnp
from jax import lax
from jax.experimental import pallas as pl
from jax.experimental.pallas import tpu as pltpu
from jax.sharding import Mesh, PartitionSpec as P

AXES = ("y", "zl", "x", "zh", "core")
SIZES = (8, 6, 4, 2, 2)
NX = 4
STEPS = 4
F32 = jnp.float32
BF16 = jnp.bfloat16
HERE = pl.BlockSpec(memory_space=pltpu.VMEM)
SMEM = pl.BlockSpec(memory_space=pltpu.SMEM)


def send(block, move):
    pairs = []
    for i, place in enumerate(np.ndindex(*SIZES)):
        goal = [a % b for a, b in zip(move(*place), SIZES)]
        pairs.append((i, int(np.ravel_multi_index(goal, SIZES))))
    return lax.ppermute(block, AXES, pairs)


def flip(block):
    return send(block, lambda y, zl, x, zh, c: (y, zl, x, 1 - zh, c))


def swap_cores(block):
    return send(block, lambda y, zl, x, zh, c: (y, zl, x, zh, 1 - c))


def next_row(y, zl, x, zh, c):
    step = 1 if c == 0 else -1
    z = (zh * 6 + zl + step) % 12
    row = zl + step
    y = y + 1 if row > 5 else y - 1 if row < 0 else y
    return (y, z % 6, x, z // 6, c)


def along_dp(block, s):
    def move(y, zl, x, zh, c):
        to = x + s if c == 0 else x - s
        if not 0 <= to < NX:
            y, zl, x, zh, c = next_row(y, zl, x, zh, c)
        return (y, zl, to, zh, c)

    return send(block, move)


def call(kernel, numbers, arrays, out_shape, flops, scratch=()):
    moved = sum(x.size * x.dtype.itemsize for x in (*arrays, *out_shape))
    return pl.pallas_call(
        kernel,
        in_specs=[SMEM] * len(numbers) + [HERE] * len(arrays),
        out_specs=[HERE] * len(out_shape),
        out_shape=out_shape,
        scratch_shapes=scratch,
        compiler_params=pltpu.CompilerParams(vmem_limit_bytes=16 * 2**20),
        cost_estimate=pl.CostEstimate(flops=flops, bytes_accessed=moved, transcendentals=0),
    )(*numbers, *arrays)


def dot(a, b):
    return jnp.dot(a, b, preferred_element_type=F32)


def halves(y, x):
    k = y.shape[2]
    return dot(y[0], x[0:k]) + dot(y[1], x[k : 2 * k])


def grad_term(x, weights):
    return lax.dot_general(x, weights, (((1,), (1,)), ((), ())), preferred_element_type=F32)


def near_kernel(info, ya, yb, x1, x2, x3, logits, yt):
    yt[0], yt[1] = ya[...].T, yb[...].T
    for m, x in enumerate((x1, x2, x3), 1):

        @pl.when(info[m] == 0)
        def _():
            logits[m - 1] = halves(yt, x)


def own_kernel(scalars, yt, yc, xa, xb, xc, keep, give, yct):
    k, r = xa.shape
    yct[0], yct[1] = yc[k : 2 * k].T, yc[0:k].T
    logits = dot(yt[0], xa[...]) + dot(yt[1], xb[...]) + halves(yct, xc)
    lined = lax.broadcasted_iota(jnp.int32, (r, r), 0)
    column = lax.broadcasted_iota(jnp.int32, (r, r), 1)
    value = jax.nn.sigmoid(scalars[0] * logits + scalars[1]) - jnp.where(lined == column, 1.0, 0.0)
    weights = (scalars[0] * value).astype(BF16)
    keep[...] = grad_term(xa[...], weights)
    give[...] = grad_term(xb[...], weights)


def block_kernel(m, info, scalars, near, yt, yct, near_x, far_x, *refs):
    n = 1 if len(refs) == 4 else 2
    before, totals, logits = refs[:n], refs[n : 2 * n], refs[-1]
    k = yt.shape[2]

    @pl.when(info[m] == 0)
    def _():
        logits[...] = near[m - 1] + halves(yct, far_x)

    @pl.when(info[m] == 1)
    def _():
        logits[...] = halves(yct, near_x) + halves(yt, far_x)

    weights = (scalars[0] * jax.nn.sigmoid(scalars[0] * logits[...] + scalars[1])).astype(BF16)
    if n == 1:
        refs[2][...] = weights
    for i, (old, total) in enumerate(zip(before, totals)):
        rows = pl.ds(k if i == 0 else 0, k)

        @pl.when(info[m] == 0)
        def _():
            total[...] = old[...] + grad_term(near_x[rows, :], weights)

        @pl.when(info[m] == 1)
        def _():
            total[...] = old[...] + grad_term(far_x[rows, :], weights)


def keep_kernel(m, info, weights, near_x, far_x, before, total):
    k = total.shape[0]

    @pl.when(info[m] == 0)
    def _():
        total[...] = before[...] + grad_term(near_x[0:k], weights[...])

    @pl.when(info[m] == 1)
    def _():
        total[...] = before[...] + grad_term(far_x[0:k], weights[...])


def on_device(image_embed, text_embed, logit_scale, logit_bias):
    place = lax.axis_index("x")
    row = lax.axis_index("zl")
    core = lax.axis_index("core")
    text, image = text_embed.T, image_embed.T
    k, r = text.shape
    xa = jnp.where(core == 0, text, image)
    ya = jnp.where(core == 0, image, text)
    with jax.named_scope("cross_a"):
        xca = flip(xa)
    with jax.named_scope("share"):
        other = swap_cores(jnp.concatenate([ya, xa], axis=0))
    xb, yb = other[:k], other[k:]
    with jax.named_scope("cross_b"):
        xcb = flip(xb)
    own = jnp.concatenate([xa, xb], axis=0)
    near_x = []
    for s in range(1, STEPS):
        with jax.named_scope("near"):
            near_x.append(along_dp(own, s))
    xc = jnp.concatenate([xca, xcb], axis=0)
    far_x = [xc]
    for s in range(1, STEPS):
        with jax.named_scope("far"):
            far_x.append(along_dp(xc, s))
    with jax.named_scope("share_far"):
        yc = swap_cores(xc)

    came = [jnp.where(core == 0, place - s < 0, place + s >= NX) for s in range(STEPS)]
    edge = jnp.where(core == 0, row == 0, row == 5)
    info = jnp.stack([jnp.logical_and(c, edge) for c in came]).astype(jnp.int32)
    scalars = jnp.concatenate([logit_scale, logit_bias])
    square, turned = jax.ShapeDtypeStruct((r, r), BF16), jax.ShapeDtypeStruct((2, r, k), BF16)
    half = jax.ShapeDtypeStruct((k, r), F32)
    work = 2 * k * r * r
    near, yt = call(
        near_kernel,
        [info],
        [ya, yb, *near_x],
        [jax.ShapeDtypeStruct((STEPS - 1, r, r), F32), turned],
        6 * work,
    )
    keep, give, yct = call(own_kernel, [scalars], [yt, yc, xa, xb, xc], [half, half, turned], 6 * work)
    for m in (3, 2):
        give, keep = call(
            functools.partial(block_kernel, m),
            [info, scalars],
            [near, yt, yct, near_x[m - 1], far_x[m], give, keep],
            [half, half],
            4 * work,
            [pltpu.VMEM((r, r), F32)],
        )
    give, weights = call(
        functools.partial(block_kernel, 1),
        [info, scalars],
        [near, yt, yct, near_x[0], far_x[1], give],
        [half, square],
        3 * work,
        [pltpu.VMEM((r, r), F32)],
    )
    with jax.named_scope("give"):
        got = swap_cores(give)
    (keep,) = call(
        functools.partial(keep_kernel, 1), [info], [weights, near_x[0], far_x[1], keep], [half], work
    )
    image_grad = jnp.where(core == 0, keep, got)
    text_grad = jnp.where(core == 0, got, keep)
    return (image_grad.T, text_grad.T)


def solution(mesh):
    split = Mesh(mesh.devices.reshape(SIZES), AXES)
    block = P(("y", "zl", "x"), ("zh", "core"))
    return jax.shard_map(
        on_device, mesh=split, in_specs=(block, block, P(), P()), out_specs=(block, block), check_vma=False
    )
```

time: 97.2 us -> 93.3 us (0.960)
  local copies, waits for them, and re-layouts: 2.67 us -> 0.11 us
  Pallas kernels: 9.17 us -> 11.3 us
  waiting for transfers between devices: 10.6 us -> 8.85 us
  starting transfers between devices: 68.9 us -> 67.3 us
    pallas_call x3 -> x6, Pallas kernels: 9.17 us -> 11.3 us  [call(): pl.pallas_call(kernel, in_specs=[SMEM] * len(numbers) + [HERE] * len(arra...]
    unnamed x7 -> x1, local copies, waits for them, and re-layouts: 1.9 us -> 0.02 us
    ppermute x11, waiting for transfers between devices: 10.6 us -> 8.85 us  [send(): return lax.ppermute(block, AXES, pairs)]
    ppermute x11, starting transfers between devices: 68.9 us -> 67.3 us  [send(): return lax.ppermute(block, AXES, pairs)]
  transfers between devices with their start and end apart: 11 -> 11, of which waited for: 2 -> 2; matrix products, arithmetic and copies ran while one was open for 2% -> 1% of each run, Pallas kernels for 5% -> 11%
where the time goes in v3:
time: 93.3 us; the launch traced here: 92.8 us
  starting transfers between devices  67.3 us (72%)
  Pallas kernels  11.3 us (12%)
  waiting for transfers between devices  8.85 us (9%)
  other arithmetic  3.07 us (3%)
  between operations  2.2 us (2%)
    ppermute x11, starting transfers between devices, send(): return lax.ppermute(block, AXES, pairs)  67.3 us
    pallas_call x6, Pallas kernels, call(): pl.pallas_call(kernel, in_specs=[SMEM] * len(numbers) + [HERE] * len(arra...  11.3 us
    ppermute x11, waiting for transfers between devices, send(): return lax.ppermute(block, AXES, pairs)  8.85 us
  transfers between devices with their start and end apart: 11, of which 2 were waited for; matrix products, arithmetic and copies ran while one was open for 1% of the time, Pallas kernels for 11%

profile of v3, /device:TPU:1, one launch (start us, length us, event | category | flops | bytes accessed | tf_op | source)
XLA Modules:
  0.0 92.8 jit_solution(7038242801149263268)
XLA Ops:
  0.6 1.1 %select_bitcast_fusion.2 = (bf16[288,384]{1,0:T(8,128)(2,1)S(1)}, bf16[288,384]{1,0:T(8,128)(2,1)S(1)}) fusion(bf16[384,288]{0,1:T(8,128)(2,1)} %param.5, bf16[384,288]{0,1:T(8,128)(2,1)} %param.4, pred[]{:T(512)S(6)} %eq.6), kind=kLoop, calls=%fused_computation.4 | loop fusion | flops 221184 | bytes 884737 | tf_op jit(solution)/shard_map/jit(_where)/select_n | solution.py:148
  1.8 12.4 %collective-permute-start = (bf16[576,384]{1,0:T(8,128)(2,1)S(1)}, bf16[576,384]{1,0:T(8,128)(2,1)S(1)}, u32[]{:S(2)}, u32[]{:S(2)}) collective-permute-start(bf16[576,384]{1,0:T(8,128)(2,1)S(1)} %pad_maximum_fusion), channel_id=1, source_target_pairs={{0,1},{1,0},{2,3},{3,2},{4,5},{5,4},{6,7},{7,6},{8,9},{9,8},{10,11... | collective-permute-start | bytes 1327112 | tf_op jit(solution)/shard_map/share/ppermute | solution.py:26
  14.2 5.8 %collective-permute-start.4 = (bf16[288,384]{1,0:T(8,128)(2,1)S(1)}, bf16[288,384]{1,0:T(8,128)(2,1)S(1)}, u32[]{:S(2)}, u32[]{:S(2)}) collective-permute-start(bf16[288,384]{1,0:T(8,128)(2,1)S(1)} %get-tuple-element.28.xa), channel_id=1, source_target_pairs={{0,2},{1,3},{2,0},{3,1},{4,6},{5,7},{6,4},{7,5},{8,10},{9,11},{10,... | collective-permute-start | bytes 663560 | tf_op jit(solution)/shard_map/cross_a/ppermute | solution.py:26
  20.1 0.0 collective-permute-done
  20.1 0.8 pad_maximum_fusion.1
  20.9 7.0 %collective-permute-start.1 = (bf16[576,384]{1,0:T(8,128)(2,1)}, bf16[576,384]{1,0:T(8,128)(2,1)S(1)}, u32[]{:S(2)}, u32[]{:S(2)}) collective-permute-start(bf16[576,384]{1,0:T(8,128)(2,1)} %pad_maximum_fusion.1), channel_id=1, source_target_pairs={{0,4},{1,767},{2,6},{3,765},{4,8},{5,1},{6,10},{7,3},{8,12},{9,5},... | collective-permute-start | bytes 1327112 | tf_op jit(solution)/shard_map/near/ppermute | solution.py:26
  27.9 8.5 %collective-permute-start.5 = (bf16[288,384]{1,0:T(8,128)(2,1)S(1)}, bf16[288,384]{1,0:T(8,128)(2,1)S(1)}, u32[]{:S(2)}, u32[]{:S(2)}) collective-permute-start(bf16[288,384]{1,0:T(8,128)(2,1)S(1)} %get-tuple-element.26.xb), channel_id=1, source_target_pairs={{0,2},{1,3},{2,0},{3,1},{4,6},{5,7},{6,4},{7,5},{8,10},{9,11},{10,... | collective-permute-start | bytes 663560 | tf_op jit(solution)/shard_map/cross_b/ppermute | solution.py:26
  36.5 3.0 %collective-permute-start.2 = (bf16[576,384]{1,0:T(8,128)(2,1)}, bf16[576,384]{1,0:T(8,128)(2,1)S(1)}, u32[]{:S(2)}, u32[]{:S(2)}) collective-permute-start(bf16[576,384]{1,0:T(8,128)(2,1)} %pad_maximum_fusion.1), channel_id=1, source_target_pairs={{0,8},{1,763},{2,10},{3,761},{4,12},{5,767},{6,14},{7,765},{8,16},... | collective-permute-start | bytes 1327112 | tf_op jit(solution)/shard_map/near/ppermute | solution.py:26
  39.5 0.0 collective-permute-done.4
  39.6 4.1 %collective-permute-start.3 = (bf16[576,384]{1,0:T(8,128)(2,1)}, bf16[576,384]{1,0:T(8,128)(2,1)S(1)}, u32[]{:S(2)}, u32[]{:S(2)}) collective-permute-start(bf16[576,384]{1,0:T(8,128)(2,1)} %pad_maximum_fusion.1), channel_id=1, source_target_pairs={{0,12},{1,759},{2,14},{3,757},{4,16},{5,763},{6,18},{7,761},{8,20}... | collective-permute-start | bytes 1327112 | tf_op jit(solution)/shard_map/near/ppermute | solution.py:26
  43.7 7.9 %collective-permute-done.5 = bf16[288,384]{1,0:T(8,128)(2,1)S(1)} collective-permute-done((bf16[288,384]{1,0:T(8,128)(2,1)S(1)}, bf16[288,384]{1,0:T(8,128)(2,1)S(1)}, u32[]{:S(2)}, u32[]{:S(2)}) %collective-permute-start.5) | collective-permute-done | bytes 221216 | tf_op jit(solution)/shard_map/cross_b/ppermute | solution.py:26
  51.7 2.3 %collective-permute-start.6 = (bf16[576,384]{1,0:T(8,128)(2,1)S(1)}, bf16[576,384]{1,0:T(8,128)(2,1)}, u32[]{:S(2)}, u32[]{:S(2)}) collective-permute-start(bf16[576,384]{1,0:T(8,128)(2,1)S(1)} %constant_dynamic-update-slice_fusion.xc), channel_id=1, source_target_pairs={{0,1},{1,0},{2,3},{3,2},{4,5},{5,4},{6,7},{7,6},{8,9},{9,8},{10,11... | collective-permute-start | bytes 1327112 | tf_op jit(solution)/shard_map/share_far/ppermute | solution.py:26
  54.0 7.3 %collective-permute-start.9 = (bf16[576,384]{1,0:T(8,128)(2,1)S(1)}, bf16[576,384]{1,0:T(8,128)(2,1)}, u32[]{:S(2)}, u32[]{:S(2)}) collective-permute-start(bf16[576,384]{1,0:T(8,128)(2,1)S(1)} %constant_dynamic-update-slice_fusion.xc), channel_id=1, source_target_pairs={{0,12},{1,759},{2,14},{3,757},{4,16},{5,763},{6,18},{7,761},{8,20}... | collective-permute-start | bytes 1327112 | tf_op jit(solution)/shard_map/far/ppermute | solution.py:26
  61.3 0.0 collective-permute-done.1.x1.near_x
  61.3 12.9 %collective-permute-start.8 = (bf16[576,384]{1,0:T(8,128)(2,1)S(1)}, bf16[576,384]{1,0:T(8,128)(2,1)S(1)}, u32[]{:S(2)}, u32[]{:S(2)}) collective-permute-start(bf16[576,384]{1,0:T(8,128)(2,1)S(1)} %constant_dynamic-update-slice_fusion.xc), channel_id=1, source_target_pairs={{0,8},{1,763},{2,10},{3,761},{4,12},{5,767},{6,14},{7,765},{8,16},... | collective-permute-start | bytes 1327112 | tf_op jit(solution)/shard_map/far/ppermute | solution.py:26
  74.2 0.0 collective-permute-done.2.x2.near_x
  74.2 1.9 %collective-permute-start.7 = (bf16[576,384]{1,0:T(8,128)(2,1)S(1)}, bf16[576,384]{1,0:T(8,128)(2,1)S(1)}, u32[]{:S(2)}, u32[]{:S(2)}) collective-permute-start(bf16[576,384]{1,0:T(8,128)(2,1)S(1)} %constant_dynamic-update-slice_fusion.xc), channel_id=1, source_target_pairs={{0,4},{1,767},{2,6},{3,765},{4,8},{5,1},{6,10},{7,3},{8,12},{9,5},... | collective-permute-start | bytes 1327112 | tf_op jit(solution)/shard_map/far/ppermute | solution.py:26
  77.5 0.1 pad_maximum_fusion.2.scalars
  77.5 0.1 add_convert_fusion.info
  77.6 0.0 collective-permute-done.3.x3.near_x
  77.6 2.3 %shard_map.59 = (f32[3,384,384]{2,1,0:T(8,128)S(1)}, bf16[2,384,288]{2,1,0:T(8,128)(2,1)S(1)}) custom-call(s32[4]{0:T(128)S(1)} %add_convert_fusion.info, bf16[288,384]{1,0:T(8,128)(2,1)S(1)} %get-tuple-element.29.ya, bf16[288,384]{1,0:T(8,128)(2,1)S(1)} %get-tuple-element.27.yb, bf16[576,384]{1,0:T(8,128)(2,1)S(1)} %collective-permute-done.1.x1.near_x, ...), custom_call_target="tpu_custom_call" | custom-call | flops 509607936 | bytes 3981312 | tf_op jit(solution)/shard_map/pallas_call | solution.py:57
  79.9 0.0 collective-permute-done.6.yc
  79.9 2.5 %shard_map.60 = (f32[288,384]{1,0:T(8,128)S(1)}, f32[288,384]{1,0:T(8,128)S(1)}, bf16[2,384,288]{2,1,0:T(8,128)(2,1)S(1)}) custom-call(f32[2]{0:T(128)S(1)} %pad_maximum_fusion.2.scalars, bf16[2,384,288]{2,1,0:T(8,128)(2,1)S(1)} %get-tuple-element.14.yt, bf16[576,384]{1,0:T(8,128)(2,1)} %collective-permute-done.6.yc, ...), custom_call_target="tpu_custom_call" | custom-call | flops 509607936 | bytes 3096576 | tf_op jit(solution)/shard_map/pallas_call | solution.py:57
  82.4 0.0 collective-permute-done.9.far_x
  82.4 2.3 %shard_map.61 = (f32[288,384]{1,0:T(8,128)S(1)}, f32[288,384]{1,0:T(8,128)S(1)}) custom-call(s32[4]{0:T(128)S(1)} %add_convert_fusion.info, f32[2]{0:T(128)S(1)} %pad_maximum_fusion.2.scalars, f32[3,384,384]{2,1,0:T(8,128)S(1)} %get-tuple-element.13.near, bf16[2,384,288]{2,1,0:T(8,128)(2,1)S(1)} %get-tuple-element.14.yt, ...), custom_call_target="tpu_custom_call" | custom-call | flops 339738624 | bytes 5308416 | tf_op jit(solution)/shard_map/pallas_call | solution.py:57
  84.8 0.0 collective-permute-done.8.far_x
  84.8 1.8 %shard_map.62 = (f32[288,384]{1,0:T(8,128)S(1)}, f32[288,384]{1,0:T(8,128)S(1)}) custom-call(s32[4]{0:T(128)S(1)} %add_convert_fusion.info, f32[2]{0:T(128)S(1)} %pad_maximum_fusion.2.scalars, f32[3,384,384]{2,1,0:T(8,128)S(1)} %get-tuple-element.13.near, bf16[2,384,288]{2,1,0:T(8,128)(2,1)S(1)} %get-tuple-element.14.yt, ...), custom_call_target="tpu_custom_call" | custom-call | flops 339738624 | bytes 5308416 | tf_op jit(solution)/shard_map/pallas_call | solution.py:57
  86.6 1.5 %shard_map.63 = (f32[288,384]{1,0:T(8,128)S(1)}, bf16[384,384]{1,0:T(8,128)(2,1)S(1)}) custom-call(s32[4]{0:T(128)S(1)} %add_convert_fusion.info, f32[2]{0:T(128)S(1)} %pad_maximum_fusion.2.scalars, f32[3,384,384]{2,1,0:T(8,128)S(1)} %get-tuple-element.13.near, bf16[2,384,288]{2,1,0:T(8,128)(2,1)S(1)} %get-tuple-element.14.yt, ...), custom_call_target="tpu_custom_call" | custom-call | flops 254803968 | bytes 4718592 | tf_op jit(solution)/shard_map/pallas_call | solution.py:57
  88.1 1.9 %collective-permute-start.10 = (f32[288,384]{1,0:T(8,128)S(1)}, f32[288,384]{1,0:T(8,128)S(1)}, u32[]{:S(2)}, u32[]{:S(2)}) collective-permute-start(f32[288,384]{1,0:T(8,128)S(1)} %get-tuple-element.23), channel_id=1, source_target_pairs={{0,1},{1,0},{2,3},{3,2},{4,5},{5,4},{6,7},{7,6},{8,9},{9,8},{10,11... | collective-permute-start | bytes 1327112 | tf_op jit(solution)/shard_map/give/ppermute | solution.py:26
  90.1 0.9 shard_map.64
  90.9 0.9 collective-permute-done.10
  91.8 1.0 %select_bitcast_fusion = (f32[384,288]{0,1:T(8,128)}, f32[384,288]{0,1:T(8,128)}) fusion(f32[288,384]{1,0:T(8,128)S(1)} %collective-permute-done.10, f32[288,384]{1,0:T(8,128)S(1)} %shard_map.64, pred[]{:T(512)S(6)} %eq.6), kind=kLoop, calls=%fused_computation.2 | loop fusion | flops 221184 | bytes 1769473 | tf_op jit(solution)/shard_map/transpose | solution.py:209
  (5 shorter events, 0.2 us)
Async XLA Ops:
  1.8 18.3 %collective-permute-start = (bf16[576,384]{1,0:T(8,128)(2,1)S(1)}, bf16[576,384]{1,0:T(8,128)(2,1)S(1)}, u32[]{:S(2)}, u32[]{:S(2)}) collective-permute-start(bf16[576,384]{1,0:T(8,128)(2,1)S(1)} %pad_maximum_fusion), channel_id=1, source_target_pairs={{0,1},{1,0},{2,3},{3,2},{4,5},{5,4},{6,7},{7,6},{8,9},{9,8},{10,11... | collective-permute-start | bytes 1327112 | tf_op jit(solution)/shard_map/share/ppermute | solution.py:26
  14.2 25.3 %collective-permute-start.4 = (bf16[288,384]{1,0:T(8,128)(2,1)S(1)}, bf16[288,384]{1,0:T(8,128)(2,1)S(1)}, u32[]{:S(2)}, u32[]{:S(2)}) collective-permute-start(bf16[288,384]{1,0:T(8,128)(2,1)S(1)} %get-tuple-element.28.xa), channel_id=1, source_target_pairs={{0,2},{1,3},{2,0},{3,1},{4,6},{5,7},{6,4},{7,5},{8,10},{9,11},{10,... | collective-permute-start | bytes 663560 | tf_op jit(solution)/shard_map/cross_a/ppermute | solution.py:26
  20.9 40.4 %collective-permute-start.1 = (bf16[576,384]{1,0:T(8,128)(2,1)}, bf16[576,384]{1,0:T(8,128)(2,1)S(1)}, u32[]{:S(2)}, u32[]{:S(2)}) collective-permute-start(bf16[576,384]{1,0:T(8,128)(2,1)} %pad_maximum_fusion.1), channel_id=1, source_target_pairs={{0,4},{1,767},{2,6},{3,765},{4,8},{5,1},{6,10},{7,3},{8,12},{9,5},... | collective-permute-start | bytes 1327112 | tf_op jit(solution)/shard_map/near/ppermute | solution.py:26
  27.9 23.7 %collective-permute-start.5 = (bf16[288,384]{1,0:T(8,128)(2,1)S(1)}, bf16[288,384]{1,0:T(8,128)(2,1)S(1)}, u32[]{:S(2)}, u32[]{:S(2)}) collective-permute-start(bf16[288,384]{1,0:T(8,128)(2,1)S(1)} %get-tuple-element.26.xb), channel_id=1, source_target_pairs={{0,2},{1,3},{2,0},{3,1},{4,6},{5,7},{6,4},{7,5},{8,10},{9,11},{10,... | collective-permute-start | bytes 663560 | tf_op jit(solution)/shard_map/cross_b/ppermute | solution.py:26
  36.5 37.7 %collective-permute-start.2 = (bf16[576,384]{1,0:T(8,128)(2,1)}, bf16[576,384]{1,0:T(8,128)(2,1)S(1)}, u32[]{:S(2)}, u32[]{:S(2)}) collective-permute-start(bf16[576,384]{1,0:T(8,128)(2,1)} %pad_maximum_fusion.1), channel_id=1, source_target_pairs={{0,8},{1,763},{2,10},{3,761},{4,12},{5,767},{6,14},{7,765},{8,16},... | collective-permute-start | bytes 1327112 | tf_op jit(solution)/shard_map/near/ppermute | solution.py:26
  39.6 38.0 %collective-permute-start.3 = (bf16[576,384]{1,0:T(8,128)(2,1)}, bf16[576,384]{1,0:T(8,128)(2,1)S(1)}, u32[]{:S(2)}, u32[]{:S(2)}) collective-permute-start(bf16[576,384]{1,0:T(8,128)(2,1)} %pad_maximum_fusion.1), channel_id=1, source_target_pairs={{0,12},{1,759},{2,14},{3,757},{4,16},{5,763},{6,18},{7,761},{8,20}... | collective-permute-start | bytes 1327112 | tf_op jit(solution)/shard_map/near/ppermute | solution.py:26
  51.7 28.2 %collective-permute-start.6 = (bf16[576,384]{1,0:T(8,128)(2,1)S(1)}, bf16[576,384]{1,0:T(8,128)(2,1)}, u32[]{:S(2)}, u32[]{:S(2)}) collective-permute-start(bf16[576,384]{1,0:T(8,128)(2,1)S(1)} %constant_dynamic-update-slice_fusion.xc), channel_id=1, source_target_pairs={{0,1},{1,0},{2,3},{3,2},{4,5},{5,4},{6,7},{7,6},{8,9},{9,8},{10,11... | collective-permute-start | bytes 1327112 | tf_op jit(solution)/shard_map/share_far/ppermute | solution.py:26
  54.0 28.4 %collective-permute-start.9 = (bf16[576,384]{1,0:T(8,128)(2,1)S(1)}, bf16[576,384]{1,0:T(8,128)(2,1)}, u32[]{:S(2)}, u32[]{:S(2)}) collective-permute-start(bf16[576,384]{1,0:T(8,128)(2,1)S(1)} %constant_dynamic-update-slice_fusion.xc), channel_id=1, source_target_pairs={{0,12},{1,759},{2,14},{3,757},{4,16},{5,763},{6,18},{7,761},{8,20}... | collective-permute-start | bytes 1327112 | tf_op jit(solution)/shard_map/far/ppermute | solution.py:26
  61.3 23.5 %collective-permute-start.8 = (bf16[576,384]{1,0:T(8,128)(2,1)S(1)}, bf16[576,384]{1,0:T(8,128)(2,1)S(1)}, u32[]{:S(2)}, u32[]{:S(2)}) collective-permute-start(bf16[576,384]{1,0:T(8,128)(2,1)S(1)} %constant_dynamic-update-slice_fusion.xc), channel_id=1, source_target_pairs={{0,8},{1,763},{2,10},{3,761},{4,12},{5,767},{6,14},{7,765},{8,16},... | collective-permute-start | bytes 1327112 | tf_op jit(solution)/shard_map/far/ppermute | solution.py:26
  74.2 12.4 %collective-permute-start.7 = (bf16[576,384]{1,0:T(8,128)(2,1)S(1)}, bf16[576,384]{1,0:T(8,128)(2,1)S(1)}, u32[]{:S(2)}, u32[]{:S(2)}) collective-permute-start(bf16[576,384]{1,0:T(8,128)(2,1)S(1)} %constant_dynamic-update-slice_fusion.xc), channel_id=1, source_target_pairs={{0,4},{1,767},{2,6},{3,765},{4,8},{5,1},{6,10},{7,3},{8,12},{9,5},... | collective-permute-start | bytes 1327112 | tf_op jit(solution)/shard_map/far/ppermute | solution.py:26
  88.1 3.7 %collective-permute-start.10 = (f32[288,384]{1,0:T(8,128)S(1)}, f32[288,384]{1,0:T(8,128)S(1)}, u32[]{:S(2)}, u32[]{:S(2)}) collective-permute-start(f32[288,384]{1,0:T(8,128)S(1)} %get-tuple-element.23), channel_id=1, source_target_pairs={{0,1},{1,0},{2,3},{3,2},{4,5},{5,4},{6,7},{7,6},{8,9},{9,8},{10,11... | collective-permute-start | bytes 1327112 | tf_op jit(solution)/shard_map/give/ppermute | solution.py:26

commit v4 on v3

--- a/solution.py
+++ b/solution.py
@@ -150,7 +150,7 @@
     with jax.named_scope("cross_a"):
         xca = flip(xa)
     with jax.named_scope("share"):
-        other = swap_cores(jnp.concatenate([ya, xa], axis=0))
+        other = lax.cond(place >= 0, swap_cores, lambda b: b, jnp.concatenate([ya, xa], axis=0))
     xb, yb = other[:k], other[k:]
     with jax.named_scope("cross_b"):
         xcb = flip(xb)

time: 93.3 us -> 91 us (0.975)
  starting transfers between devices: 67.3 us -> 65.8 us
    ppermute x11, starting transfers between devices: 67.3 us -> 65.8 us  [send(): return lax.ppermute(block, AXES, pairs)]
  transfers between devices with their start and end apart: 11 -> 11, of which waited for: 2 -> 3; matrix products, arithmetic and copies ran while one was open for 1% -> 1% of each run, Pallas kernels for 11% -> 11%
where the time goes in v4:
time: 91 us; the launch traced here: 90.5 us
  starting transfers between devices  65.8 us (72%)
  Pallas kernels  11.3 us (12%)
  waiting for transfers between devices  8 us (9%)
  other arithmetic  3.07 us (3%)
  between operations  2.2 us (2%)
    ppermute x11, starting transfers between devices, send(): return lax.ppermute(block, AXES, pairs)  65.8 us
    pallas_call x6, Pallas kernels, call(): pl.pallas_call(kernel, in_specs=[SMEM] * len(numbers) + [HERE] * len(arra...  11.3 us
    ppermute x11, waiting for transfers between devices, send(): return lax.ppermute(block, AXES, pairs)  8 us
  transfers between devices with their start and end apart: 11, of which 3 were waited for; matrix products, arithmetic and copies ran while one was open for 1% of the time, Pallas kernels for 11%

profile of v4, /device:TPU:1, one launch (start us, length us, event | category | flops | bytes accessed | tf_op | source)
XLA Modules:
  0.0 90.5 jit_solution(9321075921624833285)
XLA Ops:
  0.6 1.1 %select_bitcast_fusion.2 = (bf16[288,384]{1,0:T(8,128)(2,1)S(1)}, bf16[288,384]{1,0:T(8,128)(2,1)S(1)}) fusion(bf16[384,288]{0,1:T(8,128)(2,1)} %param.7, bf16[384,288]{0,1:T(8,128)(2,1)} %param.6, pred[]{:T(512)S(6)} %eq.6), kind=kLoop, calls=%fused_computation.4 | loop fusion | flops 221184 | bytes 884737 | tf_op jit(solution)/shard_map/jit(_where)/select_n | solution.py:148
  1.7 15.7 %collective-permute-start.4 = (bf16[288,384]{1,0:T(8,128)(2,1)S(1)}, bf16[288,384]{1,0:T(8,128)(2,1)S(1)}, u32[]{:S(2)}, u32[]{:S(2)}) collective-permute-start(bf16[288,384]{1,0:T(8,128)(2,1)S(1)} %get-tuple-element.41.xa), channel_id=1, source_target_pairs={{0,2},{1,3},{2,0},{3,1},{4,6},{5,7},{6,4},{7,5},{8,10},{9,11},{10,... | collective-permute-start | bytes 663560 | tf_op jit(solution)/shard_map/cross_a/ppermute | solution.py:26
  17.5 4.3 %conditional.1 = (bf16[576,384]{1,0:T(8,128)(2,1)S(1)}) conditional(s32[]{:T(128)} %convert_element_type.7, bf16[576,384]{1,0:T(8,128)(2,1)S(1)} %pad_maximum_fusion, bf16[576,384]{1,0:T(8,128)(2,1)S(1)} %pad_maximum_fusion), branch_computations={%region_0.1_spmd, %region_1.2_spmd} | conditional | bytes 2654256 | solution.py:153
  17.5 2.9 %collective-permute-start = (bf16[576,384]{1,0:T(8,128)(2,1)S(1)}, bf16[576,384]{1,0:T(8,128)(2,1)S(1)}, u32[]{:S(2)}, u32[]{:S(2)}) collective-permute-start(bf16[576,384]{1,0:T(8,128)(2,1)S(1)} %param.1), channel_id=1, source_target_pairs={{0,1},{1,0},{2,3},{3,2},{4,5},{5,4},{6,7},{7,6},{8,9},{9,8},{10,11... | collective-permute-start | bytes 1327112 | tf_op jit(solution)/shard_map/share/cond/branch_1_fun/ppermute | solution.py:26
  20.4 1.4 %collective-permute-done = bf16[576,384]{1,0:T(8,128)(2,1)S(1)} collective-permute-done((bf16[576,384]{1,0:T(8,128)(2,1)S(1)}, bf16[576,384]{1,0:T(8,128)(2,1)S(1)}, u32[]{:S(2)}, u32[]{:S(2)}) %collective-permute-start) | collective-permute-done | bytes 442400 | tf_op jit(solution)/shard_map/share/cond/branch_1_fun/ppermute | solution.py:26
  21.9 0.8 pad_maximum_fusion.1
  22.7 7.0 %collective-permute-start.1 = (bf16[576,384]{1,0:T(8,128)(2,1)}, bf16[576,384]{1,0:T(8,128)(2,1)S(1)}, u32[]{:S(2)}, u32[]{:S(2)}) collective-permute-start(bf16[576,384]{1,0:T(8,128)(2,1)} %pad_maximum_fusion.1), channel_id=1, source_target_pairs={{0,4},{1,767},{2,6},{3,765},{4,8},{5,1},{6,10},{7,3},{8,12},{9,5},... | collective-permute-start | bytes 1327112 | tf_op jit(solution)/shard_map/near/ppermute | solution.py:26
  29.7 8.5 %collective-permute-start.5 = (bf16[288,384]{1,0:T(8,128)(2,1)S(1)}, bf16[288,384]{1,0:T(8,128)(2,1)S(1)}, u32[]{:S(2)}, u32[]{:S(2)}) collective-permute-start(bf16[288,384]{1,0:T(8,128)(2,1)S(1)} %get-tuple-element.39.xb), channel_id=1, source_target_pairs={{0,2},{1,3},{2,0},{3,1},{4,6},{5,7},{6,4},{7,5},{8,10},{9,11},{10,... | collective-permute-start | bytes 663560 | tf_op jit(solution)/shard_map/cross_b/ppermute | solution.py:26
  38.2 3.0 %collective-permute-start.2 = (bf16[576,384]{1,0:T(8,128)(2,1)}, bf16[576,384]{1,0:T(8,128)(2,1)S(1)}, u32[]{:S(2)}, u32[]{:S(2)}) collective-permute-start(bf16[576,384]{1,0:T(8,128)(2,1)} %pad_maximum_fusion.1), channel_id=1, source_target_pairs={{0,8},{1,763},{2,10},{3,761},{4,12},{5,767},{6,14},{7,765},{8,16},... | collective-permute-start | bytes 1327112 | tf_op jit(solution)/shard_map/near/ppermute | solution.py:26
  41.3 2.5 %collective-permute-start.3 = (bf16[576,384]{1,0:T(8,128)(2,1)}, bf16[576,384]{1,0:T(8,128)(2,1)S(1)}, u32[]{:S(2)}, u32[]{:S(2)}) collective-permute-start(bf16[576,384]{1,0:T(8,128)(2,1)} %pad_maximum_fusion.1), channel_id=1, source_target_pairs={{0,12},{1,759},{2,14},{3,757},{4,16},{5,763},{6,18},{7,761},{8,20}... | collective-permute-start | bytes 1327112 | tf_op jit(solution)/shard_map/near/ppermute | solution.py:26
  43.8 0.0 collective-permute-done.4
  43.8 5.7 %collective-permute-done.5 = bf16[288,384]{1,0:T(8,128)(2,1)S(1)} collective-permute-done((bf16[288,384]{1,0:T(8,128)(2,1)S(1)}, bf16[288,384]{1,0:T(8,128)(2,1)S(1)}, u32[]{:S(2)}, u32[]{:S(2)}) %collective-permute-start.5) | collective-permute-done | bytes 221216 | tf_op jit(solution)/shard_map/cross_b/ppermute | solution.py:26
  49.5 1.9 %collective-permute-start.6 = (bf16[576,384]{1,0:T(8,128)(2,1)S(1)}, bf16[576,384]{1,0:T(8,128)(2,1)}, u32[]{:S(2)}, u32[]{:S(2)}) collective-permute-start(bf16[576,384]{1,0:T(8,128)(2,1)S(1)} %constant_dynamic-update-slice_fusion.xc), channel_id=1, source_target_pairs={{0,1},{1,0},{2,3},{3,2},{4,5},{5,4},{6,7},{7,6},{8,9},{9,8},{10,11... | collective-permute-start | bytes 1327112 | tf_op jit(solution)/shard_map/share_far/ppermute | solution.py:26
  51.5 7.0 %collective-permute-start.9 = (bf16[576,384]{1,0:T(8,128)(2,1)S(1)}, bf16[576,384]{1,0:T(8,128)(2,1)}, u32[]{:S(2)}, u32[]{:S(2)}) collective-permute-start(bf16[576,384]{1,0:T(8,128)(2,1)S(1)} %constant_dynamic-update-slice_fusion.xc), channel_id=1, source_target_pairs={{0,12},{1,759},{2,14},{3,757},{4,16},{5,763},{6,18},{7,761},{8,20}... | collective-permute-start | bytes 1327112 | tf_op jit(solution)/shard_map/far/ppermute | solution.py:26
  58.5 0.0 collective-permute-done.1.x1.near_x
  58.5 13.4 %collective-permute-start.8 = (bf16[576,384]{1,0:T(8,128)(2,1)S(1)}, bf16[576,384]{1,0:T(8,128)(2,1)S(1)}, u32[]{:S(2)}, u32[]{:S(2)}) collective-permute-start(bf16[576,384]{1,0:T(8,128)(2,1)S(1)} %constant_dynamic-update-slice_fusion.xc), channel_id=1, source_target_pairs={{0,8},{1,763},{2,10},{3,761},{4,12},{5,767},{6,14},{7,765},{8,16},... | collective-permute-start | bytes 1327112 | tf_op jit(solution)/shard_map/far/ppermute | solution.py:26
  71.9 0.0 collective-permute-done.2.x2.near_x
  71.9 1.9 %collective-permute-start.7 = (bf16[576,384]{1,0:T(8,128)(2,1)S(1)}, bf16[576,384]{1,0:T(8,128)(2,1)S(1)}, u32[]{:S(2)}, u32[]{:S(2)}) collective-permute-start(bf16[576,384]{1,0:T(8,128)(2,1)S(1)} %constant_dynamic-update-slice_fusion.xc), channel_id=1, source_target_pairs={{0,4},{1,767},{2,6},{3,765},{4,8},{5,1},{6,10},{7,3},{8,12},{9,5},... | collective-permute-start | bytes 1327112 | tf_op jit(solution)/shard_map/far/ppermute | solution.py:26
  75.2 0.1 pad_maximum_fusion.2.scalars
  75.2 0.1 add_convert_fusion.info
  75.3 0.0 collective-permute-done.3.x3.near_x
  75.3 2.3 %shard_map.59 = (f32[3,384,384]{2,1,0:T(8,128)S(1)}, bf16[2,384,288]{2,1,0:T(8,128)(2,1)S(1)}) custom-call(s32[4]{0:T(128)S(1)} %add_convert_fusion.info, bf16[288,384]{1,0:T(8,128)(2,1)S(1)} %get-tuple-element.42.ya, bf16[288,384]{1,0:T(8,128)(2,1)S(1)} %get-tuple-element.40.yb, bf16[576,384]{1,0:T(8,128)(2,1)S(1)} %collective-permute-done.1.x1.near_x, ...), custom_call_target="tpu_custom_call" | custom-call | flops 509607936 | bytes 3981312 | tf_op jit(solution)/shard_map/pallas_call | solution.py:57
  77.6 0.0 collective-permute-done.6.yc
  77.6 2.5 %shard_map.60 = (f32[288,384]{1,0:T(8,128)S(1)}, f32[288,384]{1,0:T(8,128)S(1)}, bf16[2,384,288]{2,1,0:T(8,128)(2,1)S(1)}) custom-call(f32[2]{0:T(128)S(1)} %pad_maximum_fusion.2.scalars, bf16[2,384,288]{2,1,0:T(8,128)(2,1)S(1)} %get-tuple-element.27.yt, bf16[576,384]{1,0:T(8,128)(2,1)} %collective-permute-done.6.yc, ...), custom_call_target="tpu_custom_call" | custom-call | flops 509607936 | bytes 3096576 | tf_op jit(solution)/shard_map/pallas_call | solution.py:57
  80.2 2.3 %shard_map.61 = (f32[288,384]{1,0:T(8,128)S(1)}, f32[288,384]{1,0:T(8,128)S(1)}) custom-call(s32[4]{0:T(128)S(1)} %add_convert_fusion.info, f32[2]{0:T(128)S(1)} %pad_maximum_fusion.2.scalars, f32[3,384,384]{2,1,0:T(8,128)S(1)} %get-tuple-element.26.near, bf16[2,384,288]{2,1,0:T(8,128)(2,1)S(1)} %get-tuple-element.27.yt, ...), custom_call_target="tpu_custom_call" | custom-call | flops 339738624 | bytes 5308416 | tf_op jit(solution)/shard_map/pallas_call | solution.py:57
  82.5 0.0 collective-permute-done.8.far_x
  82.5 1.8 %shard_map.62 = (f32[288,384]{1,0:T(8,128)S(1)}, f32[288,384]{1,0:T(8,128)S(1)}) custom-call(s32[4]{0:T(128)S(1)} %add_convert_fusion.info, f32[2]{0:T(128)S(1)} %pad_maximum_fusion.2.scalars, f32[3,384,384]{2,1,0:T(8,128)S(1)} %get-tuple-element.26.near, bf16[2,384,288]{2,1,0:T(8,128)(2,1)S(1)} %get-tuple-element.27.yt, ...), custom_call_target="tpu_custom_call" | custom-call | flops 339738624 | bytes 5308416 | tf_op jit(solution)/shard_map/pallas_call | solution.py:57
  84.3 1.5 %shard_map.63 = (f32[288,384]{1,0:T(8,128)S(1)}, bf16[384,384]{1,0:T(8,128)(2,1)S(1)}) custom-call(s32[4]{0:T(128)S(1)} %add_convert_fusion.info, f32[2]{0:T(128)S(1)} %pad_maximum_fusion.2.scalars, f32[3,384,384]{2,1,0:T(8,128)S(1)} %get-tuple-element.26.near, bf16[2,384,288]{2,1,0:T(8,128)(2,1)S(1)} %get-tuple-element.27.yt, ...), custom_call_target="tpu_custom_call" | custom-call | flops 254803968 | bytes 4718592 | tf_op jit(solution)/shard_map/pallas_call | solution.py:57
  85.8 1.9 %collective-permute-start.10 = (f32[288,384]{1,0:T(8,128)S(1)}, f32[288,384]{1,0:T(8,128)S(1)}, u32[]{:S(2)}, u32[]{:S(2)}) collective-permute-start(f32[288,384]{1,0:T(8,128)S(1)} %get-tuple-element.36), channel_id=1, source_target_pairs={{0,1},{1,0},{2,3},{3,2},{4,5},{5,4},{6,7},{7,6},{8,9},{9,8},{10,11... | collective-permute-start | bytes 1327112 | tf_op jit(solution)/shard_map/give/ppermute | solution.py:26
  87.8 0.9 shard_map.64
  88.6 0.9 collective-permute-done.10
  89.5 1.0 %select_bitcast_fusion = (f32[384,288]{0,1:T(8,128)}, f32[384,288]{0,1:T(8,128)}) fusion(f32[288,384]{1,0:T(8,128)S(1)} %collective-permute-done.10, f32[288,384]{1,0:T(8,128)S(1)} %shard_map.64, pred[]{:T(512)S(6)} %eq.6), kind=kLoop, calls=%fused_computation.2 | loop fusion | flops 221184 | bytes 1769473 | tf_op jit(solution)/shard_map/transpose | solution.py:209
  (7 shorter events, 0.2 us)
Async XLA Ops:
  1.7 42.0 %collective-permute-start.4 = (bf16[288,384]{1,0:T(8,128)(2,1)S(1)}, bf16[288,384]{1,0:T(8,128)(2,1)S(1)}, u32[]{:S(2)}, u32[]{:S(2)}) collective-permute-start(bf16[288,384]{1,0:T(8,128)(2,1)S(1)} %get-tuple-element.41.xa), channel_id=1, source_target_pairs={{0,2},{1,3},{2,0},{3,1},{4,6},{5,7},{6,4},{7,5},{8,10},{9,11},{10,... | collective-permute-start | bytes 663560 | tf_op jit(solution)/shard_map/cross_a/ppermute | solution.py:26
  17.5 4.3 %collective-permute-start = (bf16[576,384]{1,0:T(8,128)(2,1)S(1)}, bf16[576,384]{1,0:T(8,128)(2,1)S(1)}, u32[]{:S(2)}, u32[]{:S(2)}) collective-permute-start(bf16[576,384]{1,0:T(8,128)(2,1)S(1)} %param.1), channel_id=1, source_target_pairs={{0,1},{1,0},{2,3},{3,2},{4,5},{5,4},{6,7},{7,6},{8,9},{9,8},{10,11... | collective-permute-start | bytes 1327112 | tf_op jit(solution)/shard_map/share/cond/branch_1_fun/ppermute | solution.py:26
  22.7 35.8 %collective-permute-start.1 = (bf16[576,384]{1,0:T(8,128)(2,1)}, bf16[576,384]{1,0:T(8,128)(2,1)S(1)}, u32[]{:S(2)}, u32[]{:S(2)}) collective-permute-start(bf16[576,384]{1,0:T(8,128)(2,1)} %pad_maximum_fusion.1), channel_id=1, source_target_pairs={{0,4},{1,767},{2,6},{3,765},{4,8},{5,1},{6,10},{7,3},{8,12},{9,5},... | collective-permute-start | bytes 1327112 | tf_op jit(solution)/shard_map/near/ppermute | solution.py:26
  29.7 19.8 %collective-permute-start.5 = (bf16[288,384]{1,0:T(8,128)(2,1)S(1)}, bf16[288,384]{1,0:T(8,128)(2,1)S(1)}, u32[]{:S(2)}, u32[]{:S(2)}) collective-permute-start(bf16[288,384]{1,0:T(8,128)(2,1)S(1)} %get-tuple-element.39.xb), channel_id=1, source_target_pairs={{0,2},{1,3},{2,0},{3,1},{4,6},{5,7},{6,4},{7,5},{8,10},{9,11},{10,... | collective-permute-start | bytes 663560 | tf_op jit(solution)/shard_map/cross_b/ppermute | solution.py:26
  38.2 33.7 %collective-permute-start.2 = (bf16[576,384]{1,0:T(8,128)(2,1)}, bf16[576,384]{1,0:T(8,128)(2,1)S(1)}, u32[]{:S(2)}, u32[]{:S(2)}) collective-permute-start(bf16[576,384]{1,0:T(8,128)(2,1)} %pad_maximum_fusion.1), channel_id=1, source_target_pairs={{0,8},{1,763},{2,10},{3,761},{4,12},{5,767},{6,14},{7,765},{8,16},... | collective-permute-start | bytes 1327112 | tf_op jit(solution)/shard_map/near/ppermute | solution.py:26
  41.3 34.1 %collective-permute-start.3 = (bf16[576,384]{1,0:T(8,128)(2,1)}, bf16[576,384]{1,0:T(8,128)(2,1)S(1)}, u32[]{:S(2)}, u32[]{:S(2)}) collective-permute-start(bf16[576,384]{1,0:T(8,128)(2,1)} %pad_maximum_fusion.1), channel_id=1, source_target_pairs={{0,12},{1,759},{2,14},{3,757},{4,16},{5,763},{6,18},{7,761},{8,20}... | collective-permute-start | bytes 1327112 | tf_op jit(solution)/shard_map/near/ppermute | solution.py:26
  49.5 28.1 %collective-permute-start.6 = (bf16[576,384]{1,0:T(8,128)(2,1)S(1)}, bf16[576,384]{1,0:T(8,128)(2,1)}, u32[]{:S(2)}, u32[]{:S(2)}) collective-permute-start(bf16[576,384]{1,0:T(8,128)(2,1)S(1)} %constant_dynamic-update-slice_fusion.xc), channel_id=1, source_target_pairs={{0,1},{1,0},{2,3},{3,2},{4,5},{5,4},{6,7},{7,6},{8,9},{9,8},{10,11... | collective-permute-start | bytes 1327112 | tf_op jit(solution)/shard_map/share_far/ppermute | solution.py:26
  51.5 28.7 %collective-permute-start.9 = (bf16[576,384]{1,0:T(8,128)(2,1)S(1)}, bf16[576,384]{1,0:T(8,128)(2,1)}, u32[]{:S(2)}, u32[]{:S(2)}) collective-permute-start(bf16[576,384]{1,0:T(8,128)(2,1)S(1)} %constant_dynamic-update-slice_fusion.xc), channel_id=1, source_target_pairs={{0,12},{1,759},{2,14},{3,757},{4,16},{5,763},{6,18},{7,761},{8,20}... | collective-permute-start | bytes 1327112 | tf_op jit(solution)/shard_map/far/ppermute | solution.py:26
  58.5 24.0 %collective-permute-start.8 = (bf16[576,384]{1,0:T(8,128)(2,1)S(1)}, bf16[576,384]{1,0:T(8,128)(2,1)S(1)}, u32[]{:S(2)}, u32[]{:S(2)}) collective-permute-start(bf16[576,384]{1,0:T(8,128)(2,1)S(1)} %constant_dynamic-update-slice_fusion.xc), channel_id=1, source_target_pairs={{0,8},{1,763},{2,10},{3,761},{4,12},{5,767},{6,14},{7,765},{8,16},... | collective-permute-start | bytes 1327112 | tf_op jit(solution)/shard_map/far/ppermute | solution.py:26
  71.9 12.4 %collective-permute-start.7 = (bf16[576,384]{1,0:T(8,128)(2,1)S(1)}, bf16[576,384]{1,0:T(8,128)(2,1)S(1)}, u32[]{:S(2)}, u32[]{:S(2)}) collective-permute-start(bf16[576,384]{1,0:T(8,128)(2,1)S(1)} %constant_dynamic-update-slice_fusion.xc), channel_id=1, source_target_pairs={{0,4},{1,767},{2,6},{3,765},{4,8},{5,1},{6,10},{7,3},{8,12},{9,5},... | collective-permute-start | bytes 1327112 | tf_op jit(solution)/shard_map/far/ppermute | solution.py:26
  85.8 3.7 %collective-permute-start.10 = (f32[288,384]{1,0:T(8,128)S(1)}, f32[288,384]{1,0:T(8,128)S(1)}, u32[]{:S(2)}, u32[]{:S(2)}) collective-permute-start(f32[288,384]{1,0:T(8,128)S(1)} %get-tuple-element.36), channel_id=1, source_target_pairs={{0,1},{1,0},{2,3},{3,2},{4,5},{5,4},{6,7},{7,6},{8,9},{9,8},{10,11... | collective-permute-start | bytes 1327112 | tf_op jit(solution)/shard_map/give/ppermute | solution.py:26

commit v5 on v4

--- a/solution.py
+++ b/solution.py
@@ -26,6 +26,10 @@
     return lax.ppermute(block, AXES, pairs)
 
 
+def after(value, other):
+    return lax.optimization_barrier((value, other))[0]
+
+
 def flip(block):
     return send(block, lambda y, zl, x, zh, c: (y, zl, x, 1 - zh, c))
 
@@ -60,7 +64,7 @@
         out_specs=[HERE] * len(out_shape),
         out_shape=out_shape,
         scratch_shapes=scratch,
-        compiler_params=pltpu.CompilerParams(vmem_limit_bytes=16 * 2**20),
+        compiler_params=pltpu.CompilerParams(vmem_limit_bytes=8 * 2**20),
         cost_estimate=pl.CostEstimate(flops=flops, bytes_accessed=moved, transcendentals=0),
     )(*numbers, *arrays)
 
@@ -165,7 +169,7 @@
         with jax.named_scope("far"):
             far_x.append(along_dp(xc, s))
     with jax.named_scope("share_far"):
-        yc = swap_cores(xc)
+        yc = swap_cores(after(xc, near_x[0]))
 
     came = [jnp.where(core == 0, place - s < 0, place + s >= NX) for s in range(STEPS)]
     edge = jnp.where(core == 0, row == 0, row == 5)
@@ -182,7 +186,8 @@
         6 * work,
     )
     keep, give, yct = call(own_kernel, [scalars], [yt, yc, xa, xb, xc], [half, half, turned], 6 * work)
-    for m in (3, 2):
+    *others, last = 3, 2, 1
+    for m in others:
         give, keep = call(
             functools.partial(block_kernel, m),
             [info, scalars],
@@ -192,9 +197,9 @@
             [pltpu.VMEM((r, r), F32)],
         )
     give, weights = call(
-        functools.partial(block_kernel, 1),
+        functools.partial(block_kernel, last),
         [info, scalars],
-        [near, yt, yct, near_x[0], far_x[1], give],
+        [near, yt, yct, near_x[last - 1], far_x[last], give],
         [half, square],
         3 * work,
         [pltpu.VMEM((r, r), F32)],
@@ -202,7 +207,7 @@
     with jax.named_scope("give"):
         got = swap_cores(give)
     (keep,) = call(
-        functools.partial(keep_kernel, 1), [info], [weights, near_x[0], far_x[1], keep], [half], work
+        functools.partial(keep_kernel, last), [info], [weights, near_x[last - 1], far_x[last], keep], [half], work
     )
     image_grad = jnp.where(core == 0, keep, got)
     text_grad = jnp.where(core == 0, got, keep)

time: 91 us -> 91 us (level)
  no operation moved by 1% of the time
where the time goes in v5:
time: 91 us; the launch traced here: 90.5 us
  starting transfers between devices  65.8 us (72%)
  Pallas kernels  11.3 us (12%)
  waiting for transfers between devices  8 us (9%)
  other arithmetic  3.06 us (3%)
  between operations  2.2 us (2%)
    ppermute x11, starting transfers between devices, send(): return lax.ppermute(block, AXES, pairs)  65.8 us
    pallas_call x6, Pallas kernels, call(): pl.pallas_call(kernel, in_specs=[SMEM] * len(numbers) + [HERE] * len(arra...  11.3 us
    ppermute x11, waiting for transfers between devices, send(): return lax.ppermute(block, AXES, pairs)  8 us
  transfers between devices with their start and end apart: 11, of which 3 were waited for; matrix products, arithmetic and copies ran while one was open for 1% of the time, Pallas kernels for 11%

profile of v5, /device:TPU:1, one launch (start us, length us, event | category | flops | bytes accessed | tf_op | source)
XLA Modules:
  0.0 90.5 jit_solution(12407501716381419883)
XLA Ops:
  0.6 1.1 %select_bitcast_fusion.2 = (bf16[288,384]{1,0:T(8,128)(2,1)S(1)}, bf16[288,384]{1,0:T(8,128)(2,1)S(1)}) fusion(bf16[384,288]{0,1:T(8,128)(2,1)} %param.7, bf16[384,288]{0,1:T(8,128)(2,1)} %param.6, pred[]{:T(512)S(6)} %eq.6), kind=kLoop, calls=%fused_computation.4 | loop fusion | flops 221184 | bytes 884737 | tf_op jit(solution)/shard_map/jit(_where)/select_n | solution.py:152
  1.7 15.7 %collective-permute-start.4 = (bf16[288,384]{1,0:T(8,128)(2,1)S(1)}, bf16[288,384]{1,0:T(8,128)(2,1)S(1)}, u32[]{:S(2)}, u32[]{:S(2)}) collective-permute-start(bf16[288,384]{1,0:T(8,128)(2,1)S(1)} %get-tuple-element.43.xa), channel_id=1, source_target_pairs={{0,2},{1,3},{2,0},{3,1},{4,6},{5,7},{6,4},{7,5},{8,10},{9,11},{10,... | collective-permute-start | bytes 663560 | tf_op jit(solution)/shard_map/cross_a/ppermute | solution.py:26
  17.5 4.3 %conditional.1 = (bf16[576,384]{1,0:T(8,128)(2,1)S(1)}) conditional(s32[]{:T(128)} %convert_element_type.7, bf16[576,384]{1,0:T(8,128)(2,1)S(1)} %pad_maximum_fusion, bf16[576,384]{1,0:T(8,128)(2,1)S(1)} %pad_maximum_fusion), branch_computations={%region_0.1_spmd, %region_1.2_spmd} | conditional | bytes 2654256 | solution.py:157
  17.5 2.9 %collective-permute-start = (bf16[576,384]{1,0:T(8,128)(2,1)S(1)}, bf16[576,384]{1,0:T(8,128)(2,1)S(1)}, u32[]{:S(2)}, u32[]{:S(2)}) collective-permute-start(bf16[576,384]{1,0:T(8,128)(2,1)S(1)} %param.1), channel_id=1, source_target_pairs={{0,1},{1,0},{2,3},{3,2},{4,5},{5,4},{6,7},{7,6},{8,9},{9,8},{10,11... | collective-permute-start | bytes 1327112 | tf_op jit(solution)/shard_map/share/cond/branch_1_fun/ppermute | solution.py:26
  20.4 1.4 %collective-permute-done = bf16[576,384]{1,0:T(8,128)(2,1)S(1)} collective-permute-done((bf16[576,384]{1,0:T(8,128)(2,1)S(1)}, bf16[576,384]{1,0:T(8,128)(2,1)S(1)}, u32[]{:S(2)}, u32[]{:S(2)}) %collective-permute-start) | collective-permute-done | bytes 442400 | tf_op jit(solution)/shard_map/share/cond/branch_1_fun/ppermute | solution.py:26
  21.9 0.8 pad_maximum_fusion.1
  22.7 7.0 %collective-permute-start.1 = (bf16[576,384]{1,0:T(8,128)(2,1)}, bf16[576,384]{1,0:T(8,128)(2,1)S(1)}, u32[]{:S(2)}, u32[]{:S(2)}) collective-permute-start(bf16[576,384]{1,0:T(8,128)(2,1)} %pad_maximum_fusion.1), channel_id=1, source_target_pairs={{0,4},{1,767},{2,6},{3,765},{4,8},{5,1},{6,10},{7,3},{8,12},{9,5},... | collective-permute-start | bytes 1327112 | tf_op jit(solution)/shard_map/near/ppermute | solution.py:26
  29.7 8.5 %collective-permute-start.5 = (bf16[288,384]{1,0:T(8,128)(2,1)S(1)}, bf16[288,384]{1,0:T(8,128)(2,1)S(1)}, u32[]{:S(2)}, u32[]{:S(2)}) collective-permute-start(bf16[288,384]{1,0:T(8,128)(2,1)S(1)} %get-tuple-element.41.xb), channel_id=1, source_target_pairs={{0,2},{1,3},{2,0},{3,1},{4,6},{5,7},{6,4},{7,5},{8,10},{9,11},{10,... | collective-permute-start | bytes 663560 | tf_op jit(solution)/shard_map/cross_b/ppermute | solution.py:26
  38.2 3.0 %collective-permute-start.2 = (bf16[576,384]{1,0:T(8,128)(2,1)}, bf16[576,384]{1,0:T(8,128)(2,1)S(1)}, u32[]{:S(2)}, u32[]{:S(2)}) collective-permute-start(bf16[576,384]{1,0:T(8,128)(2,1)} %pad_maximum_fusion.1), channel_id=1, source_target_pairs={{0,8},{1,763},{2,10},{3,761},{4,12},{5,767},{6,14},{7,765},{8,16},... | collective-permute-start | bytes 1327112 | tf_op jit(solution)/shard_map/near/ppermute | solution.py:26
  41.3 2.5 %collective-permute-start.3 = (bf16[576,384]{1,0:T(8,128)(2,1)}, bf16[576,384]{1,0:T(8,128)(2,1)S(1)}, u32[]{:S(2)}, u32[]{:S(2)}) collective-permute-start(bf16[576,384]{1,0:T(8,128)(2,1)} %pad_maximum_fusion.1), channel_id=1, source_target_pairs={{0,12},{1,759},{2,14},{3,757},{4,16},{5,763},{6,18},{7,761},{8,20}... | collective-permute-start | bytes 1327112 | tf_op jit(solution)/shard_map/near/ppermute | solution.py:26
  43.8 0.0 collective-permute-done.4
  43.8 5.7 %collective-permute-done.5 = bf16[288,384]{1,0:T(8,128)(2,1)S(1)} collective-permute-done((bf16[288,384]{1,0:T(8,128)(2,1)S(1)}, bf16[288,384]{1,0:T(8,128)(2,1)S(1)}, u32[]{:S(2)}, u32[]{:S(2)}) %collective-permute-start.5) | collective-permute-done | bytes 221216 | tf_op jit(solution)/shard_map/cross_b/ppermute | solution.py:26
  49.5 0.0 collective-permute-done.1.x1.near_x
  49.5 1.9 %collective-permute-start.6 = (bf16[576,384]{1,0:T(8,128)(2,1)S(1)}, bf16[576,384]{1,0:T(8,128)(2,1)}, u32[]{:S(2)}, u32[]{:S(2)}) collective-permute-start(bf16[576,384]{1,0:T(8,128)(2,1)S(1)} %constant_dynamic-update-slice_fusion.xc), channel_id=1, source_target_pairs={{0,1},{1,0},{2,3},{3,2},{4,5},{5,4},{6,7},{7,6},{8,9},{9,8},{10,11... | collective-permute-start | bytes 1327112 | tf_op jit(solution)/shard_map/share_far/ppermute | solution.py:26
  51.5 7.0 %collective-permute-start.9 = (bf16[576,384]{1,0:T(8,128)(2,1)S(1)}, bf16[576,384]{1,0:T(8,128)(2,1)}, u32[]{:S(2)}, u32[]{:S(2)}) collective-permute-start(bf16[576,384]{1,0:T(8,128)(2,1)S(1)} %constant_dynamic-update-slice_fusion.xc), channel_id=1, source_target_pairs={{0,12},{1,759},{2,14},{3,757},{4,16},{5,763},{6,18},{7,761},{8,20}... | collective-permute-start | bytes 1327112 | tf_op jit(solution)/shard_map/far/ppermute | solution.py:26
  58.5 13.4 %collective-permute-start.8 = (bf16[576,384]{1,0:T(8,128)(2,1)S(1)}, bf16[576,384]{1,0:T(8,128)(2,1)S(1)}, u32[]{:S(2)}, u32[]{:S(2)}) collective-permute-start(bf16[576,384]{1,0:T(8,128)(2,1)S(1)} %constant_dynamic-update-slice_fusion.xc), channel_id=1, source_target_pairs={{0,8},{1,763},{2,10},{3,761},{4,12},{5,767},{6,14},{7,765},{8,16},... | collective-permute-start | bytes 1327112 | tf_op jit(solution)/shard_map/far/ppermute | solution.py:26
  71.9 0.0 collective-permute-done.2.x2.near_x
  71.9 1.9 %collective-permute-start.7 = (bf16[576,384]{1,0:T(8,128)(2,1)S(1)}, bf16[576,384]{1,0:T(8,128)(2,1)S(1)}, u32[]{:S(2)}, u32[]{:S(2)}) collective-permute-start(bf16[576,384]{1,0:T(8,128)(2,1)S(1)} %constant_dynamic-update-slice_fusion.xc), channel_id=1, source_target_pairs={{0,4},{1,767},{2,6},{3,765},{4,8},{5,1},{6,10},{7,3},{8,12},{9,5},... | collective-permute-start | bytes 1327112 | tf_op jit(solution)/shard_map/far/ppermute | solution.py:26
  75.2 0.1 pad_maximum_fusion.2.scalars
  75.2 0.1 add_convert_fusion.info
  75.3 0.0 collective-permute-done.3.x3.near_x
  75.3 2.3 %shard_map.59 = (f32[3,384,384]{2,1,0:T(8,128)S(1)}, bf16[2,384,288]{2,1,0:T(8,128)(2,1)S(1)}) custom-call(s32[4]{0:T(128)S(1)} %add_convert_fusion.info, bf16[288,384]{1,0:T(8,128)(2,1)S(1)} %get-tuple-element.44.ya, bf16[288,384]{1,0:T(8,128)(2,1)S(1)} %get-tuple-element.42.yb, bf16[576,384]{1,0:T(8,128)(2,1)S(1)} %collective-permute-done.1.x1.near_x, ...), custom_call_target="tpu_custom_call" | custom-call | flops 509607936 | bytes 3981312 | tf_op jit(solution)/shard_map/pallas_call | solution.py:61
  77.6 0.0 collective-permute-done.6.yc
  77.6 2.5 %shard_map.60 = (f32[288,384]{1,0:T(8,128)S(1)}, f32[288,384]{1,0:T(8,128)S(1)}, bf16[2,384,288]{2,1,0:T(8,128)(2,1)S(1)}) custom-call(f32[2]{0:T(128)S(1)} %pad_maximum_fusion.2.scalars, bf16[2,384,288]{2,1,0:T(8,128)(2,1)S(1)} %get-tuple-element.28.yt, bf16[576,384]{1,0:T(8,128)(2,1)} %collective-permute-done.6.yc, ...), custom_call_target="tpu_custom_call" | custom-call | flops 509607936 | bytes 3096576 | tf_op jit(solution)/shard_map/pallas_call | solution.py:61
  80.1 0.0 collective-permute-done.9.far_x
  80.2 2.3 %shard_map.61 = (f32[288,384]{1,0:T(8,128)S(1)}, f32[288,384]{1,0:T(8,128)S(1)}) custom-call(s32[4]{0:T(128)S(1)} %add_convert_fusion.info, f32[2]{0:T(128)S(1)} %pad_maximum_fusion.2.scalars, f32[3,384,384]{2,1,0:T(8,128)S(1)} %get-tuple-element.27.near, bf16[2,384,288]{2,1,0:T(8,128)(2,1)S(1)} %get-tuple-element.28.yt, ...), custom_call_target="tpu_custom_call" | custom-call | flops 339738624 | bytes 5308416 | tf_op jit(solution)/shard_map/pallas_call | solution.py:61
  82.5 1.8 %shard_map.62 = (f32[288,384]{1,0:T(8,128)S(1)}, f32[288,384]{1,0:T(8,128)S(1)}) custom-call(s32[4]{0:T(128)S(1)} %add_convert_fusion.info, f32[2]{0:T(128)S(1)} %pad_maximum_fusion.2.scalars, f32[3,384,384]{2,1,0:T(8,128)S(1)} %get-tuple-element.27.near, bf16[2,384,288]{2,1,0:T(8,128)(2,1)S(1)} %get-tuple-element.28.yt, ...), custom_call_target="tpu_custom_call" | custom-call | flops 339738624 | bytes 5308416 | tf_op jit(solution)/shard_map/pallas_call | solution.py:61
  84.3 1.5 %shard_map.63 = (f32[288,384]{1,0:T(8,128)S(1)}, bf16[384,384]{1,0:T(8,128)(2,1)S(1)}) custom-call(s32[4]{0:T(128)S(1)} %add_convert_fusion.info, f32[2]{0:T(128)S(1)} %pad_maximum_fusion.2.scalars, f32[3,384,384]{2,1,0:T(8,128)S(1)} %get-tuple-element.27.near, bf16[2,384,288]{2,1,0:T(8,128)(2,1)S(1)} %get-tuple-element.28.yt, ...), custom_call_target="tpu_custom_call" | custom-call | flops 254803968 | bytes 4718592 | tf_op jit(solution)/shard_map/pallas_call | solution.py:61
  85.8 1.9 %collective-permute-start.10 = (f32[288,384]{1,0:T(8,128)S(1)}, f32[288,384]{1,0:T(8,128)S(1)}, u32[]{:S(2)}, u32[]{:S(2)}) collective-permute-start(f32[288,384]{1,0:T(8,128)S(1)} %get-tuple-element.38), channel_id=1, source_target_pairs={{0,1},{1,0},{2,3},{3,2},{4,5},{5,4},{6,7},{7,6},{8,9},{9,8},{10,11... | collective-permute-start | bytes 1327112 | tf_op jit(solution)/shard_map/give/ppermute | solution.py:26
  87.8 0.9 shard_map.64
  88.6 0.9 collective-permute-done.10
  89.5 1.0 %select_bitcast_fusion = (f32[384,288]{0,1:T(8,128)}, f32[384,288]{0,1:T(8,128)}) fusion(f32[288,384]{1,0:T(8,128)S(1)} %collective-permute-done.10, f32[288,384]{1,0:T(8,128)S(1)} %shard_map.64, pred[]{:T(512)S(6)} %eq.6), kind=kLoop, calls=%fused_computation.2 | loop fusion | flops 221184 | bytes 1769473 | tf_op jit(solution)/shard_map/transpose | solution.py:214
  (7 shorter events, 0.2 us)
Async XLA Ops:
  1.7 42.0 %collective-permute-start.4 = (bf16[288,384]{1,0:T(8,128)(2,1)S(1)}, bf16[288,384]{1,0:T(8,128)(2,1)S(1)}, u32[]{:S(2)}, u32[]{:S(2)}) collective-permute-start(bf16[288,384]{1,0:T(8,128)(2,1)S(1)} %get-tuple-element.43.xa), channel_id=1, source_target_pairs={{0,2},{1,3},{2,0},{3,1},{4,6},{5,7},{6,4},{7,5},{8,10},{9,11},{10,... | collective-permute-start | bytes 663560 | tf_op jit(solution)/shard_map/cross_a/ppermute | solution.py:26
  17.5 4.3 %collective-permute-start = (bf16[576,384]{1,0:T(8,128)(2,1)S(1)}, bf16[576,384]{1,0:T(8,128)(2,1)S(1)}, u32[]{:S(2)}, u32[]{:S(2)}) collective-permute-start(bf16[576,384]{1,0:T(8,128)(2,1)S(1)} %param.1), channel_id=1, source_target_pairs={{0,1},{1,0},{2,3},{3,2},{4,5},{5,4},{6,7},{7,6},{8,9},{9,8},{10,11... | collective-permute-start | bytes 1327112 | tf_op jit(solution)/shard_map/share/cond/branch_1_fun/ppermute | solution.py:26
  22.7 26.9 %collective-permute-start.1 = (bf16[576,384]{1,0:T(8,128)(2,1)}, bf16[576,384]{1,0:T(8,128)(2,1)S(1)}, u32[]{:S(2)}, u32[]{:S(2)}) collective-permute-start(bf16[576,384]{1,0:T(8,128)(2,1)} %pad_maximum_fusion.1), channel_id=1, source_target_pairs={{0,4},{1,767},{2,6},{3,765},{4,8},{5,1},{6,10},{7,3},{8,12},{9,5},... | collective-permute-start | bytes 1327112 | tf_op jit(solution)/shard_map/near/ppermute | solution.py:26
  29.7 19.8 %collective-permute-start.5 = (bf16[288,384]{1,0:T(8,128)(2,1)S(1)}, bf16[288,384]{1,0:T(8,128)(2,1)S(1)}, u32[]{:S(2)}, u32[]{:S(2)}) collective-permute-start(bf16[288,384]{1,0:T(8,128)(2,1)S(1)} %get-tuple-element.41.xb), channel_id=1, source_target_pairs={{0,2},{1,3},{2,0},{3,1},{4,6},{5,7},{6,4},{7,5},{8,10},{9,11},{10,... | collective-permute-start | bytes 663560 | tf_op jit(solution)/shard_map/cross_b/ppermute | solution.py:26
  38.2 33.7 %collective-permute-start.2 = (bf16[576,384]{1,0:T(8,128)(2,1)}, bf16[576,384]{1,0:T(8,128)(2,1)S(1)}, u32[]{:S(2)}, u32[]{:S(2)}) collective-permute-start(bf16[576,384]{1,0:T(8,128)(2,1)} %pad_maximum_fusion.1), channel_id=1, source_target_pairs={{0,8},{1,763},{2,10},{3,761},{4,12},{5,767},{6,14},{7,765},{8,16},... | collective-permute-start | bytes 1327112 | tf_op jit(solution)/shard_map/near/ppermute | solution.py:26
  41.3 34.1 %collective-permute-start.3 = (bf16[576,384]{1,0:T(8,128)(2,1)}, bf16[576,384]{1,0:T(8,128)(2,1)S(1)}, u32[]{:S(2)}, u32[]{:S(2)}) collective-permute-start(bf16[576,384]{1,0:T(8,128)(2,1)} %pad_maximum_fusion.1), channel_id=1, source_target_pairs={{0,12},{1,759},{2,14},{3,757},{4,16},{5,763},{6,18},{7,761},{8,20}... | collective-permute-start | bytes 1327112 | tf_op jit(solution)/shard_map/near/ppermute | solution.py:26
  49.5 28.1 %collective-permute-start.6 = (bf16[576,384]{1,0:T(8,128)(2,1)S(1)}, bf16[576,384]{1,0:T(8,128)(2,1)}, u32[]{:S(2)}, u32[]{:S(2)}) collective-permute-start(bf16[576,384]{1,0:T(8,128)(2,1)S(1)} %constant_dynamic-update-slice_fusion.xc), channel_id=1, source_target_pairs={{0,1},{1,0},{2,3},{3,2},{4,5},{5,4},{6,7},{7,6},{8,9},{9,8},{10,11... | collective-permute-start | bytes 1327112 | tf_op jit(solution)/shard_map/share_far/ppermute | solution.py:26
  51.5 28.7 %collective-permute-start.9 = (bf16[576,384]{1,0:T(8,128)(2,1)S(1)}, bf16[576,384]{1,0:T(8,128)(2,1)}, u32[]{:S(2)}, u32[]{:S(2)}) collective-permute-start(bf16[576,384]{1,0:T(8,128)(2,1)S(1)} %constant_dynamic-update-slice_fusion.xc), channel_id=1, source_target_pairs={{0,12},{1,759},{2,14},{3,757},{4,16},{5,763},{6,18},{7,761},{8,20}... | collective-permute-start | bytes 1327112 | tf_op jit(solution)/shard_map/far/ppermute | solution.py:26
  58.5 24.0 %collective-permute-start.8 = (bf16[576,384]{1,0:T(8,128)(2,1)S(1)}, bf16[576,384]{1,0:T(8,128)(2,1)S(1)}, u32[]{:S(2)}, u32[]{:S(2)}) collective-permute-start(bf16[576,384]{1,0:T(8,128)(2,1)S(1)} %constant_dynamic-update-slice_fusion.xc), channel_id=1, source_target_pairs={{0,8},{1,763},{2,10},{3,761},{4,12},{5,767},{6,14},{7,765},{8,16},... | collective-permute-start | bytes 1327112 | tf_op jit(solution)/shard_map/far/ppermute | solution.py:26
  71.9 12.4 %collective-permute-start.7 = (bf16[576,384]{1,0:T(8,128)(2,1)S(1)}, bf16[576,384]{1,0:T(8,128)(2,1)S(1)}, u32[]{:S(2)}, u32[]{:S(2)}) collective-permute-start(bf16[576,384]{1,0:T(8,128)(2,1)S(1)} %constant_dynamic-update-slice_fusion.xc), channel_id=1, source_target_pairs={{0,4},{1,767},{2,6},{3,765},{4,8},{5,1},{6,10},{7,3},{8,12},{9,5},... | collective-permute-start | bytes 1327112 | tf_op jit(solution)/shard_map/far/ppermute | solution.py:26
  85.8 3.7 %collective-permute-start.10 = (f32[288,384]{1,0:T(8,128)S(1)}, f32[288,384]{1,0:T(8,128)S(1)}, u32[]{:S(2)}, u32[]{:S(2)}) collective-permute-start(f32[288,384]{1,0:T(8,128)S(1)} %get-tuple-element.38), channel_id=1, source_target_pairs={{0,1},{1,0},{2,3},{3,2},{4,5},{5,4},{6,7},{7,6},{8,9},{9,8},{10,11... | collective-permute-start | bytes 1327112 | tf_op jit(solution)/shard_map/give/ppermute | solution.py:26
